TPU v7x, 256 devices: a whole 4x4x8 slice. The times are simulated.
256 devices in a mesh: dp: 32 (over z_hi, y, core), cls: 8 (over x, z_lo).
Axes of the slice: x: 4, y: 4, z: 8 (z_hi: 4, z_lo: 2; z = z_hi * 2 + z_lo), core: 2. Of those that a mesh axis runs over, the one named last changes fastest.
Arguments:
- features: bfloat16 [16384, 1024], P('dp'), may hold values from -6 to 6
- labels: int32 [16384], P('dp'), may hold values from 0 to 11263
- inducing: bfloat16 [2048, 1024], P('cls'), may hold values from -6 to 6
- mean_weights: bfloat16 [2048, 11264], P('dp', 'cls'), may hold values from -0.125 to 0.125
- class_variance: float32 [11264], P('cls'), may hold values from 0.25 to 4
- class_rate: float32 [11264], P('cls'), may hold values from 0.2 to 10, as said below
Outputs:
- first_stats: float32 [2048, 11264], P('dp', 'cls')
- second_stats: float32 [2048, 11264], P('dp', 'cls')
Inputs may be any that keep to these rules, and one draw needn't show every extreme that they name: `class_rate`: positive class weights.
All inputs are finite; a program needn't handle non-finite values.
Results may differ from a plain program's by a relative error of at most 0.0049.
Values may be sent and summed in bfloat16 or wider, within the bound.
No kernel may reach another device: no remote copies, remote signals or barrier semaphores. Data moves between devices by JAX's collectives and lax.ppermute only.
A program may use at most 128 MiB of HBM per device.

v0:
```python
import jax
import jax.numpy as jnp
from jax import lax
from jax.experimental import pallas as pl
from jax.experimental.pallas import tpu as pltpu
from jax.sharding import Mesh, PartitionSpec as P

SIZE = {"g": 2, "h": 2, "y": 4, "c": 2, "x": 4, "zl": 2}
AXES = tuple(SIZE)
BF = jnp.bfloat16
F32 = jnp.float32
SLAB = 128
ORDER = (0, 1, 3, 2)
PART = 128


def swap(value, zh=0, **masks):
    if zh:
        masks = dict(masks, g=zh // 2, h=zh % 2)
    masks = {a: m for a, m in masks.items() if m}
    names = tuple(a for a in AXES if a in masks)
    pairs, count = [], 1
    for a in names:
        count *= SIZE[a]
    for i in range(count):
        left, at = i, {}
        for a in reversed(names):
            at[a] = left % SIZE[a]
            left //= SIZE[a]
        j = 0
        for a in names:
            j = j * SIZE[a] + (at[a] ^ masks[a])
        pairs.append((i, j))
    return lax.ppermute(value, names, pairs)


def normalized(rows):
    values = rows.astype(F32)
    scale = lax.rsqrt(jnp.mean(values * values, axis=-1, keepdims=True) + 1e-06)
    return (values * scale).astype(BF)


def vmem_call(body, name, out_shape, given, scratch=(), flops=0, smem=0):
    vmem = pl.BlockSpec(memory_space=pltpu.VMEM)
    moved = sum(v.size * v.dtype.itemsize for v in (*given, *out_shape))
    return pl.pallas_call(
        body,
        out_shape=tuple(out_shape),
        in_specs=[pl.BlockSpec(memory_space=pltpu.SMEM)] * smem + [vmem] * (len(given) - smem),
        out_specs=(vmem,) * len(out_shape),
        scratch_shapes=list(scratch),
        compiler_params=pltpu.CompilerParams(vmem_limit_bytes=48 << 20),
        cost_estimate=pl.CostEstimate(flops=flops, bytes_accessed=moved, transcendentals=0),
        name=name,
    )(*given)


def slab_at(index):
    return pl.ds(pl.multiple_of(index * SLAB, SLAB), SLAB)


def write_rows(left, table, place, first, factor, out, out_sq, block):
    dots = lax.dot_general(left, table, (((1,), (1,)), ((), ())), preferred_element_type=F32)
    value = jnp.exp(dots * factor).astype(BF)
    wide = value.astype(F32)
    square = (wide * wide).astype(BF)
    for kl in range(2):
        to = slab_at(place[first + kl])
        out[block, to] = value[:, kl * SLAB : (kl + 1) * SLAB]
        out_sq[block, to] = square[:, kl * SLAB : (kl + 1) * SLAB]


def near_rows(places, features, relay, relay_far, pair, across, packs, across_packs):
    own, width = features.shape
    factor = 1.0 / float(width) ** 0.5
    step = 512

    def body(place, feature, relay, relay_far, pair, across, near, back, near_a, back_a, out, out_sq, held):
        held[pl.ds(pl.multiple_of(place[16] * own, own), own)] = normalized(feature[...])
        for k, rows in enumerate((relay, near, relay_far, back)):
            at = pl.ds(pl.multiple_of(place[12 + k] * PART, PART), PART)
            held[at] = rows[...] if k % 2 == 0 else rows[2 * SLAB :]
        tables = (pair, across, near, near_a, back, back_a)

        @pl.loop(0, 2 * own // step)
        def _(i):
            block = pl.ds(pl.multiple_of(i * step, step), step)
            for n, table in enumerate(tables):
                write_rows(held[block], table[: 2 * SLAB], place, 2 * n, factor, out, out_sq, block)

    shape = jax.ShapeDtypeStruct((2 * own, 12 * SLAB), BF)
    given = [places, features, relay, relay_far, pair, across, *packs, *across_packs]
    return vmem_call(
        body, "near_rows", (shape, shape, jax.ShapeDtypeStruct((2 * own, width), BF)), given, (), 4 * own * 12 * SLAB * width, 1
    )


def means_of(places, rows, far, far_across, near_k, ours, theirs, variance, rate):
    count, width = rows.shape
    quarter = ours[0].shape[0]
    factor = 1.0 / float(width) ** 0.5
    step, cut, cols = 256, 3 * SLAB, 4 * SLAB

    def body(place, rows, far, far_across, near_k, *refs):
        blocks, (variance, rate, out, out_sq, ratio, slope, total, weights) = refs[:8], refs[8:]
        for k in range(2):
            here = slice(k * quarter, (k + 1) * quarter)
            for ky in range(4):
                block = blocks[4 * k + ky]
                weights[here, ky * cut : (ky + 1) * cut] = block[:, :cut]
                weights[here, 12 * SLAB + ky * SLAB : 12 * SLAB + (ky + 1) * SLAB] = block[:, cut:]

        @pl.loop(0, count // 512)
        def _(i):
            block = pl.ds(pl.multiple_of(i * 512, 512), 512)
            for n, table in enumerate((far, far_across)):
                write_rows(rows[block], table[...], place, 2 * n, factor, out, out_sq, block)

        @pl.loop(0, count // step)
        def _(i):
            block = pl.ds(pl.multiple_of(i * step, step), step)
            transposed = (((1,), (1,)), ((), ()))
            for k in range(2):
                here = slice(k * quarter, (k + 1) * quarter)
                means = lax.dot_general(
                    weights[here, : 12 * SLAB], near_k[block], transposed, preferred_element_type=F32
                ) + lax.dot_general(weights[here, 12 * SLAB :], out[block], transposed, preferred_element_type=F32)
                square = means * means + variance[here]
                inverse = lax.rsqrt(square)
                spread = square * inverse
                small = jnp.exp(-spread)
                share = 1.0 / (1.0 + small)
                value = rate[here] * jnp.exp(-(means + spread) * 0.5) * share
                ratio[here, block] = value
                slope[here, block] = (1.0 - small) * share * (0.5 * inverse)
                part = jnp.sum(value, axis=0, keepdims=True)
                total[:, block] = part if k == 0 else total[:, block] + part

    wide = jax.ShapeDtypeStruct((2 * quarter, count), F32)
    last = jax.ShapeDtypeStruct((count, 4 * SLAB), BF)
    given = [places, rows, far, far_across, near_k, *ours, *theirs, variance, rate]
    return vmem_call(
        body,
        "means",
        (last, last, wide, wide, jax.ShapeDtypeStruct((1, count), F32)),
        given,
        [pltpu.VMEM((2 * quarter, 4 * cols), BF)],
        2 * count * 16 * SLAB * 2 * quarter,
        1,
    )


def statistic(which, ratio, slope, intensity, labels, ids, near, last):
    quarter, count = ratio.shape[0] // 2, ratio.shape[1]
    step = 2 * SLAB

    def body(ratio, slope, intensity, labels, ids, near, last, keep, give, weight):
        for k in range(4):
            here = slice(k * quarter // 2, (k + 1) * quarter // 2)
            hot = (ids[here] == labels[...]).astype(F32)
            expected = intensity[...] * ratio[here]
            value = (hot - expected) * 0.5 if which == 0 else (hot + expected) * slope[here]
            weight[here] = value.astype(BF)

        for source, per in ((near, 3), (last, 1)):

            @pl.loop(0, source.shape[1] // step)
            def _(j):
                block = pl.ds(pl.multiple_of(j * step, step), step)
                sums = jnp.dot(weight[...], source[:, block], preferred_element_type=F32)
                for k in range(2):
                    slab = 2 * j + k
                    ky = slab // per
                    to = slab_at(ky * 4 + (slab - ky * per if per == 3 else 3))
                    part = sums[:, k * SLAB : (k + 1) * SLAB]
                    keep[:, to] = part[:quarter]
                    give[:, to] = part[quarter:].astype(BF)

    shape = (quarter, 16 * SLAB)
    given = [ratio, slope, intensity, labels, ids, near, last]
    return vmem_call(
        body,
        "statistic",
        (jax.ShapeDtypeStruct(shape, F32), jax.ShapeDtypeStruct(shape, BF)),
        given,
        [pltpu.VMEM(ratio.shape, BF)],
        2 * count * 16 * SLAB * 2 * quarter,
    )


def body(features, labels, inducing, mean_weights, class_variance, class_rate):
    g, h, y, c, x, zl = (lax.axis_index(a) for a in AXES)
    zh = 2 * g + h
    all_local = mean_weights.shape[1]
    half = all_local // 2
    quarter = half // 2

    mine = normalized(lax.dynamic_slice_in_dim(inducing, c * SLAB, SLAB, 0))
    relay = normalized(lax.dynamic_slice_in_dim(features, x * PART, PART, 0))
    mine, relay, mean_weights = lax.optimization_barrier((mine, relay, mean_weights))
    relay = swap(relay, zh=1)
    labs = swap(labels, zh=1)
    pair = jnp.concatenate([mine, swap(mine, zl=1)], 0)

    local = mean_weights.T.reshape(2, 2, quarter, -1)
    keep = lax.dynamic_index_in_dim(local, c, 1, False)
    give = lax.dynamic_index_in_dim(local, 1 - c, 1, False)
    got = swap(give, c=1)
    block = jnp.where(c == 0, jnp.concatenate([keep, got], 2), jnp.concatenate([got, keep], 2))
    same = lax.dynamic_index_in_dim(block, h, 0, False)
    other = lax.dynamic_index_in_dim(block, 1 - h, 0, False)
    over_z = jnp.stack([same, swap(other, zh=1), swap(same, zh=2), swap(other, zh=3)])
    over_z = jnp.concatenate([lax.dynamic_index_in_dim(over_z, zh ^ x ^ kx, 0, False) for kx in ORDER], 1)

    pack = jnp.concatenate([pair, relay], 0)
    near, back = swap(pack, x=1), swap(pack, x=3)
    over_z, pack, labs = lax.optimization_barrier((over_z, pack, labs))
    over_y = [over_z, swap(over_z, y=1), None, swap(over_z, y=3)]
    relay_far, near, back, pair, over_z, over_y[1], over_y[3] = lax.optimization_barrier(
        (swap(relay, x=2), near, back, pair, over_z, over_y[1], over_y[3])
    )
    over_y[2] = swap(over_z, y=2)
    far = swap(pair, x=2)

    def places(order):
        found = []
        for i, kx in enumerate(order):
            for core in (c, 1 - c):
                for kl in range(2):
                    found.append((y ^ ((zl ^ kl) * 2 + core)) * len(order) + i)
        return found

    where = places(ORDER[:3]) + [(1 - h) * 4 + (x ^ kx) for kx in range(4)] + [h]
    where = jnp.stack(where).astype(jnp.int32)
    across = (swap(near, c=1), swap(back, c=1))
    near_k, near_sq, rows = near_rows(where, features, relay, relay_far, pair, swap(pair, c=1), (near, back), across)
    far, rows = lax.optimization_barrier((far, rows))

    def of_classes(value):
        value = lax.dynamic_slice_in_dim(value, h * half, half, 0)
        return jnp.where(c == 0, value, jnp.concatenate([value[quarter:], value[:quarter]]))[:, None]

    ids = (x * 2 + zl) * all_local + of_classes(jnp.arange(all_local, dtype=jnp.int32))
    labs = jnp.where(h == 0, jnp.concatenate([labels, labs]), jnp.concatenate([labs, labels]))[None, :]
    where = jnp.stack(places(ORDER[3:])).astype(jnp.int32)
    last_k, last_sq, ratio, slope, total = means_of(
        where, rows, far, swap(far, c=1), near_k, over_y, [swap(v, c=1) for v in over_y],
        of_classes(class_variance), of_classes(class_rate),
    )
    total = jnp.tile(total.reshape(1, 8, 128), (16, 1, 1))
    total = jnp.sum(lax.all_to_all(total, ("h", "x", "zl"), 0, 0, tiled=True), axis=0).reshape(1, -1)
    all_classes = all_local * 8
    intensity = (1.0 + total) / (1.0 + 0.5 * all_classes)

    sums = []
    for which, (near_part, last_part) in enumerate(((near_k, last_k), (near_sq, last_sq))):
        kept, give = statistic(which, ratio, slope, intensity, labs, ids, near_part, last_part)
        sums.append((kept, swap(give, c=1)))

    def chunk(which, ky):
        at = slice(ky * 512, (ky + 1) * 512)
        return sums[which][0][:, at] + sums[which][1][:, at].astype(F32)

    def over_rows(which, came):
        near, back, far = (value.astype(F32) for value in came)
        return (chunk(which, 0) + far) + (near + back)

    def slab_of(value, kz):
        kx = x ^ zh ^ kz
        return lax.dynamic_slice_in_dim(value, (kx ^ (kx // 2)) * SLAB, SLAB, 1)

    def outgoing(own):
        middle = lax.reduce_precision(jnp.mean(own, axis=1), 8, 7)
        rest = (own - middle[:, None]).astype(BF)
        tail = jnp.pad(middle.astype(BF), (0, 16 * SLAB - quarter)).reshape(16, SLAB)
        return [jnp.concatenate([slab_of(rest, kz), tail], 0) for kz in (2, 1, 3)]

    def incoming(value):
        middle = value[quarter:].reshape(-1)[:quarter]
        return value[:quarter].astype(F32) + middle.astype(F32)[:, None]

    came = [[swap(chunk(0, ky).astype(BF), y=ky) for ky in (1, 3, 2)], [swap(chunk(1, ky).astype(BF), y=ky) for ky in (1, 3)]]
    far, came[0][0] = lax.optimization_barrier((chunk(1, 2).astype(BF), came[0][0]))
    came[1].append(swap(far, y=2))
    own = over_rows(0, came[0])
    send = lax.optimization_barrier(outgoing(own))
    got = [swap(send[0], zh=2), swap(send[1], zh=1)]
    came[1], got = lax.optimization_barrier((came[1], got))
    early, late, own_early = got, send[2], own
    own = over_rows(1, came[1])
    send = lax.optimization_barrier(outgoing(own))
    both = swap(jnp.concatenate([send[2], late], 0), zh=3)
    early = early + [both[quarter + 16 :]]
    got = [swap(send[0], zh=2), swap(send[1], zh=1), both[: quarter + 16]]

    def total_of(own, got):
        got = [incoming(value) for value in got]
        return jnp.stack([slab_of(own, 0) + got[0], got[1] + got[2]])

    summed = jnp.stack([total_of(own_early, early), total_of(own, got)]) * (1.0 / (512 * 32))
    summed = summed.transpose(0, 3, 1, 2)
    mine = lax.dynamic_slice_in_dim(summed, c * 64, 64, 1)
    theirs = swap(lax.dynamic_slice_in_dim(summed, (1 - c) * 64, 64, 1), c=1)
    both = jnp.where(c == 0, jnp.stack([mine, theirs], 3), jnp.stack([theirs, mine], 3))
    both = jnp.where(h == 0, both, both[:, :, ::-1])
    out = both.reshape(2, 64, all_local)
    return out[0], out[1]


def solution(mesh):
    parts = Mesh(mesh.devices.reshape(tuple(SIZE.values())), AXES)
    dp, cls = ("g", "h", "y", "c"), ("x", "zl")
    in_specs = (P(dp, None), P(dp), P(cls, None), P(dp, cls), P(cls), P(cls))
    out_specs = (P(dp, cls), P(dp, cls))
    return jax.shard_map(body, mesh=parts, in_specs=in_specs, out_specs=out_specs, check_vma=False)
```

profile of v0, /device:TPU:1, one launch (start us, length us, event | category | flops | bytes accessed | tf_op | source)
XLA Modules:
  0.0 188.4 jit_solution(11743653785658877424)
XLA Ops:
  5.0 3.3 %collective-permute-start.5 = (bf16[2,352,64]{2,1,0:T(8,128)(2,1)S(1)}, bf16[2,352,64]{2,1,0:T(8,128)(2,1)S(1)}, u32[]{:S(2)}, u32[]{:S(2)}) collective-permute-start(bf16[2,352,64]{2,1,0:T(8,128)(2,1)S(1)} %bitcast.86), channel_id=1, source_target_pairs={{0,8},{8,0},{1,9},{9,1},{2,10},{10,2},{3,11},{11,3},{4,12},{12,4},... | collective-permute-start | bytes 270344 | tf_op jit(solution)/shard_map/ppermute | solution.py:34
  8.4 2.9 %collective-permute-start = (bf16[128,1024]{1,0:T(8,128)(2,1)S(1)}, bf16[128,1024]{1,0:T(8,128)(2,1)S(1)}, u32[]{:S(2)}, u32[]{:S(2)}) collective-permute-start(bf16[128,1024]{1,0:T(8,128)(2,1)S(1)} %get-tuple-element.41), channel_id=1, source_target_pairs={{0,64},{64,0},{1,65},{65,1},{2,66},{66,2},{3,67},{67,3},{4,68},{68... | collective-permute-start | bytes 786440 | tf_op jit(solution)/shard_map/ppermute | solution.py:34
  12.5 3.4 %collective-permute-start.8 = (bf16[352,128]{1,0:T(8,128)(2,1)S(1)}, bf16[352,128]{1,0:T(8,128)(2,1)S(1)}, u32[]{:S(2)}, u32[]{:S(2)}) collective-permute-start(bf16[352,128]{1,0:T(8,128)(2,1)S(1)} %get-tuple-element.111), channel_id=1, source_target_pairs={{0,192},{64,128},{128,64},{192,0},{1,193},{65,129},{129,65},{193,1... | collective-permute-start | bytes 270344 | tf_op jit(solution)/shard_map/ppermute | solution.py:34
  18.2 4.3 %collective-permute-done.2 = bf16[128,1024]{1,0:T(8,128)(2,1)S(1)} collective-permute-done((bf16[128,1024]{1,0:T(8,128)(2,1)S(1)}, bf16[128,1024]{1,0:T(8,128)(2,1)S(1)}, u32[]{:S(2)}, u32[]{:S(2)}) %collective-permute-start.2) | collective-permute-done | bytes 262176 | tf_op jit(solution)/shard_map/ppermute | solution.py:34
  25.6 7.6 %collective-permute-done.7 = bf16[352,128]{1,0:T(8,128)(2,1)S(1)} collective-permute-done((bf16[352,128]{1,0:T(8,128)(2,1)S(1)}, bf16[352,128]{1,0:T(8,128)(2,1)S(1)}, u32[]{:S(2)}, u32[]{:S(2)}) %collective-permute-start.7) | collective-permute-done | bytes 90144 | tf_op jit(solution)/shard_map/ppermute | solution.py:34
  33.4 3.5 %collective-permute-done.9 = s32[512]{0:T(512)S(1)} collective-permute-done((s32[512]{0:T(512)S(1)}, s32[512]{0:T(512)S(1)}, u32[]{:S(2)}, u32[]{:S(2)}) %collective-permute-start.9) | collective-permute-done | bytes 2080 | tf_op jit(solution)/shard_map/ppermute | solution.py:34
  40.1 2.3 %collective-permute-start.1 = (bf16[128,1024]{1,0:T(8,128)(2,1)S(1)}, bf16[128,1024]{1,0:T(8,128)(2,1)S(1)}, u32[]{:S(2)}, u32[]{:S(2)}) collective-permute-start(bf16[128,1024]{1,0:T(8,128)(2,1)S(1)} %collective-permute-done.relay), channel_id=1, source_target_pairs={{0,4},{2,6},{4,0},{6,2},{1,5},{3,7},{5,1},{7,3},{8,12},{10,14},{12... | collective-permute-start | bytes 786440 | tf_op jit(solution)/shard_map/ppermute | solution.py:34
  42.5 5.0 %collective-permute-done.1.relay_far = bf16[128,1024]{1,0:T(8,128)(2,1)S(1)} collective-permute-done((bf16[128,1024]{1,0:T(8,128)(2,1)S(1)}, bf16[128,1024]{1,0:T(8,128)(2,1)S(1)}, u32[]{:S(2)}, u32[]{:S(2)}) %collective-permute-start.1) | collective-permute-done | bytes 262176 | tf_op jit(solution)/shard_map/ppermute | solution.py:34
  48.3 3.2 %collective-permute-start.14 = (bf16[384,1024]{1,0:T(8,128)(2,1)S(1)}, bf16[384,1024]{1,0:T(8,128)(2,1)}, u32[]{:S(2)}, u32[]{:S(2)}) collective-permute-start(bf16[384,1024]{1,0:T(8,128)(2,1)S(1)} %collective-permute-done.3.near), channel_id=1, source_target_pairs={{0,8},{8,0},{1,9},{9,1},{2,10},{10,2},{3,11},{11,3},{4,12},{12,4},... | collective-permute-start | bytes 2359304 | tf_op jit(solution)/shard_map/ppermute | solution.py:34
  52.3 2.5 %collective-permute-start.12 = (bf16[256,1024]{1,0:T(8,128)(2,1)S(1)}, bf16[256,1024]{1,0:T(8,128)(2,1)}, u32[]{:S(2)}, u32[]{:S(2)}) collective-permute-start(bf16[256,1024]{1,0:T(8,128)(2,1)S(1)} %pad_maximum_fusion.pair), channel_id=1, source_target_pairs={{0,4},{2,6},{4,0},{6,2},{1,5},{3,7},{5,1},{7,3},{8,12},{10,14},{12... | collective-permute-start | bytes 1572872 | tf_op jit(solution)/shard_map/ppermute | solution.py:34
  57.0 10.4 %near_rows.1 = (bf16[1024,1536]{1,0:T(8,128)(2,1)}, bf16[1024,1536]{1,0:T(8,128)(2,1)}, bf16[1024,1024]{1,0:T(8,128)(2,1)}) custom-call(s32[17]{0:T(128)S(1)} %stack.149.place, bf16[512,1024]{1,0:T(8,128)(2,1)S(1)} %copy-done.1, bf16[128,1024]{1,0:T(8,128)(2,1)S(1)} %collective-permute-done.relay, bf16[128,1024]{1,0:T(8,128)(2,1)S(1)} %copy-done.3, ...), custom_call_target="tpu_custom_call" | custom-call | flops 3221225472 | bytes 14155844 | tf_op jit(solution)/shard_map/near_rows/pallas_call | solution.py:46
  72.1 13.2 %means.1 = (bf16[1024,512]{1,0:T(8,128)(2,1)S(1)}, bf16[1024,512]{1,0:T(8,128)(2,1)}, f32[704,1024]{1,0:T(8,128)}, f32[704,1024]{1,0:T(8,128)}, f32[1,1024]{1,0:T(1,128)S(1)}) custom-call(s32[4]{0:T(128)S(1)} %pad_add_fusion.place, bf16[1024,1024]{1,0:T(8,128)(2,1)} %get-tuple-element.50.rows, bf16[256,1024]{1,0:T(8,128)(2,1)} %collective-permute-done.12.far, ...), custom_call_target="tpu_custom_call" | custom-call | flops 2952790016 | bytes 17049104 | tf_op jit(solution)/shard_map/means/pallas_call | solution.py:46
  87.0 6.7 %all-to-all-start = ((f32[16,8,128]{2,1,0:T(8,128)}), f32[16,8,128]{2,1,0:T(8,128)S(1)}, u32[]{:S(2)}, u32[]{:S(2)}) async-start(f32[16,8,128]{2,1,0:T(8,128)} %tile.9), calls=%async_computation | async-start | bytes 131072 | tf_op jit(solution)/shard_map/all_to_all | solution.py:251
  94.0 6.7 %all-to-all-done = f32[16,8,128]{2,1,0:T(8,128)S(1)} async-done(((f32[16,8,128]{2,1,0:T(8,128)}), f32[16,8,128]{2,1,0:T(8,128)S(1)}, u32[]{:S(2)}, u32[]{:S(2)}) %all-to-all-start) | async-done | bytes 65568 | tf_op jit(solution)/shard_map/all_to_all | solution.py:251
  101.9 8.8 %statistic.2 = (f32[352,2048]{1,0:T(8,128)S(1)}, bf16[352,2048]{1,0:T(8,128)(2,1)S(1)}) custom-call(f32[704,1024]{1,0:T(8,128)} %get-tuple-element.56.ratio, f32[704,1024]{1,0:T(8,128)} %get-tuple-element.57.slope, f32[1,1024]{1,0:T(1,128)S(1)} %bitcast.80, s32[1,1024]{1,0:T(1,128)S(1)} %broadcast_select_fusion.labels, s32[704,1]{1,0:T(8,128)S(1)} %add.349.ids, ...), custom_call_target="tpu_custom_call" | custom-call | flops 2952790016 | bytes 14297856 | tf_op jit(solution)/shard_map/statistic/pallas_call | solution.py:46
  112.7 9.9 %statistic.3 = (f32[352,2048]{1,0:T(8,128)S(1)}, bf16[352,2048]{1,0:T(8,128)(2,1)}) custom-call(f32[704,1024]{1,0:T(8,128)} %get-tuple-element.56.ratio, f32[704,1024]{1,0:T(8,128)} %get-tuple-element.57.slope, f32[1,1024]{1,0:T(1,128)S(1)} %bitcast.81, s32[1,1024]{1,0:T(1,128)S(1)} %broadcast_select_fusion.labels, s32[704,1]{1,0:T(8,128)S(1)} %add.349.ids, ...), custom_call_target="tpu_custom_call" | custom-call | flops 2952790016 | bytes 14297856 | tf_op jit(solution)/shard_map/statistic/pallas_call | solution.py:46
  125.5 2.6 %collective-permute-start.23 = (bf16[352,512]{1,0:T(8,128)(2,1)}, bf16[352,512]{1,0:T(8,128)(2,1)}, u32[]{:S(2)}, u32[]{:S(2)}) collective-permute-start(bf16[352,512]{1,0:T(8,128)(2,1)} %get-tuple-element.87), channel_id=1, source_target_pairs={{0,32},{16,48},{32,0},{48,16},{1,33},{17,49},{33,1},{49,17},{2,34}... | collective-permute-start | bytes 1081352 | tf_op jit(solution)/shard_map/ppermute | solution.py:34
  128.9 2.4 %add_convert_fusion = (bf16[352,512]{1,0:T(8,128)(2,1)}, bf16[352,512]{1,0:T(8,128)(2,1)}, bf16[352,512]{1,0:T(8,128)(2,1)}) fusion(f32[352,2048]{1,0:T(8,128)S(1)} %get-tuple-element.65, bf16[352,2048]{1,0:T(8,128)(2,1)} %collective-permute-done.24), kind=kLoop, calls=%fused_computation.8 | loop fusion | flops 1622016 | bytes 4325376 | tf_op jit(solution)/shard_map/convert_element_type | solution.py:282
  135.3 9.4 %collective-permute-done.23 = bf16[352,512]{1,0:T(8,128)(2,1)} collective-permute-done((bf16[352,512]{1,0:T(8,128)(2,1)}, bf16[352,512]{1,0:T(8,128)(2,1)}, u32[]{:S(2)}, u32[]{:S(2)}) %collective-permute-start.23) | collective-permute-done | bytes 360480 | tf_op jit(solution)/shard_map/ppermute | solution.py:34
  150.2 6.7 %collective-permute-start.30 = (bf16[368,128]{1,0:T(8,128)(2,1)}, bf16[368,128]{1,0:T(8,128)(2,1)S(1)}, u32[]{:S(2)}, u32[]{:S(2)}) collective-permute-start(bf16[368,128]{1,0:T(8,128)(2,1)} %get-tuple-element.69), channel_id=1, source_target_pairs={{0,128},{128,0},{1,129},{129,1},{2,130},{130,2},{3,131},{131,3},{4... | collective-permute-start | bytes 282632 | tf_op jit(solution)/shard_map/ppermute | solution.py:34
  157.4 4.8 %collective-permute-done.28 = bf16[352,512]{1,0:T(8,128)(2,1)} collective-permute-done((bf16[352,512]{1,0:T(8,128)(2,1)}, bf16[352,512]{1,0:T(8,128)(2,1)}, u32[]{:S(2)}, u32[]{:S(2)}) %collective-permute-start.28) | collective-permute-done | bytes 360480 | tf_op jit(solution)/shard_map/ppermute | solution.py:34
  162.2 4.5 %collective-permute-done.31 = bf16[368,128]{1,0:T(8,128)(2,1)S(1)} collective-permute-done((bf16[368,128]{1,0:T(8,128)(2,1)}, bf16[368,128]{1,0:T(8,128)(2,1)S(1)}, u32[]{:S(2)}, u32[]{:S(2)}) %collective-permute-start.31) | collective-permute-done | bytes 94240 | tf_op jit(solution)/shard_map/ppermute | solution.py:34
  171.1 3.1 %collective-permute-start.33 = (bf16[368,128]{1,0:T(8,128)(2,1)S(1)}, bf16[368,128]{1,0:T(8,128)(2,1)S(1)}, u32[]{:S(2)}, u32[]{:S(2)}) collective-permute-start(bf16[368,128]{1,0:T(8,128)(2,1)S(1)} %get-tuple-element.78), channel_id=1, source_target_pairs={{0,128},{128,0},{1,129},{129,1},{2,130},{130,2},{3,131},{131,3},{4... | collective-permute-start | bytes 282632 | tf_op jit(solution)/shard_map/ppermute | solution.py:34
  175.2 5.6 %collective-permute-done.33 = bf16[368,128]{1,0:T(8,128)(2,1)S(1)} collective-permute-done((bf16[368,128]{1,0:T(8,128)(2,1)S(1)}, bf16[368,128]{1,0:T(8,128)(2,1)S(1)}, u32[]{:S(2)}, u32[]{:S(2)}) %collective-permute-start.33) | collective-permute-done | bytes 94240 | tf_op jit(solution)/shard_map/ppermute | solution.py:34
  (157 shorter events, 54.3 us)
Async XLA Ops:
  8.4 14.2 %collective-permute-start.2 = (bf16[128,1024]{1,0:T(8,128)(2,1)S(1)}, bf16[128,1024]{1,0:T(8,128)(2,1)S(1)}, u32[]{:S(2)}, u32[]{:S(2)}) collective-permute-start(bf16[128,1024]{1,0:T(8,128)(2,1)S(1)} %get-tuple-element.42), channel_id=1, source_target_pairs={{0,1},{1,0},{2,3},{3,2},{4,5},{5,4},{6,7},{7,6},{8,9},{9,8},{10,11... | collective-permute-start | bytes 786440 | tf_op jit(solution)/shard_map/ppermute | solution.py:34
  8.4 14.9 %collective-permute-start = (bf16[128,1024]{1,0:T(8,128)(2,1)S(1)}, bf16[128,1024]{1,0:T(8,128)(2,1)S(1)}, u32[]{:S(2)}, u32[]{:S(2)}) collective-permute-start(bf16[128,1024]{1,0:T(8,128)(2,1)S(1)} %get-tuple-element.41), channel_id=1, source_target_pairs={{0,64},{64,0},{1,65},{65,1},{2,66},{66,2},{3,67},{67,3},{4,68},{68... | collective-permute-start | bytes 786440 | tf_op jit(solution)/shard_map/ppermute | solution.py:34
  12.5 20.7 %collective-permute-start.8 = (bf16[352,128]{1,0:T(8,128)(2,1)S(1)}, bf16[352,128]{1,0:T(8,128)(2,1)S(1)}, u32[]{:S(2)}, u32[]{:S(2)}) collective-permute-start(bf16[352,128]{1,0:T(8,128)(2,1)S(1)} %get-tuple-element.111), channel_id=1, source_target_pairs={{0,192},{64,128},{128,64},{192,0},{1,193},{65,129},{129,65},{193,1... | collective-permute-start | bytes 270344 | tf_op jit(solution)/shard_map/ppermute | solution.py:34
  15.9 17.3 %collective-permute-start.6 = (bf16[352,128]{1,0:T(8,128)(2,1)S(1)}, bf16[352,128]{1,0:T(8,128)(2,1)S(1)}, u32[]{:S(2)}, u32[]{:S(2)}) collective-permute-start(bf16[352,128]{1,0:T(8,128)(2,1)S(1)} %get-tuple-element.111), channel_id=1, source_target_pairs={{0,64},{64,0},{1,65},{65,1},{2,66},{66,2},{3,67},{67,3},{4,68},{68... | collective-permute-start | bytes 270344 | tf_op jit(solution)/shard_map/ppermute | solution.py:34
  17.1 16.1 %collective-permute-start.7 = (bf16[352,128]{1,0:T(8,128)(2,1)S(1)}, bf16[352,128]{1,0:T(8,128)(2,1)S(1)}, u32[]{:S(2)}, u32[]{:S(2)}) collective-permute-start(bf16[352,128]{1,0:T(8,128)(2,1)S(1)} %bitcast.84), channel_id=1, source_target_pairs={{0,128},{128,0},{1,129},{129,1},{2,130},{130,2},{3,131},{131,3},{4... | collective-permute-start | bytes 270344 | tf_op jit(solution)/shard_map/ppermute | solution.py:34
  24.0 24.3 %collective-permute-start.3 = (bf16[384,1024]{1,0:T(8,128)(2,1)}, bf16[384,1024]{1,0:T(8,128)(2,1)S(1)}, u32[]{:S(2)}, u32[]{:S(2)}) collective-permute-start(bf16[384,1024]{1,0:T(8,128)(2,1)} %constant_dynamic-update-slice_fusion), channel_id=1, source_target_pairs={{0,2},{2,0},{4,6},{6,4},{1,3},{3,1},{5,7},{7,5},{8,10},{10,8},{12,... | collective-permute-start | bytes 2359304 | tf_op jit(solution)/shard_map/ppermute | solution.py:34
  24.0 24.3 %collective-permute-start.4 = (bf16[384,1024]{1,0:T(8,128)(2,1)}, bf16[384,1024]{1,0:T(8,128)(2,1)}, u32[]{:S(2)}, u32[]{:S(2)}) collective-permute-start(bf16[384,1024]{1,0:T(8,128)(2,1)} %constant_dynamic-update-slice_fusion), channel_id=1, source_target_pairs={{0,6},{2,4},{4,2},{6,0},{1,7},{3,5},{5,3},{7,1},{8,14},{10,12},{12... | collective-permute-start | bytes 2359304 | tf_op jit(solution)/shard_map/ppermute | solution.py:34
  36.9 11.3 %collective-permute-start.10 = (bf16[352,512]{1,0:T(8,128)(2,1)S(1)}, bf16[352,512]{1,0:T(8,128)(2,1)}, u32[]{:S(2)}, u32[]{:S(2)}) collective-permute-start(bf16[352,512]{1,0:T(8,128)(2,1)S(1)} %pad_maximum_fusion.2.refs_0_), channel_id=1, source_target_pairs={{0,16},{16,0},{32,48},{48,32},{1,17},{17,1},{33,49},{49,33},{2,18}... | collective-permute-start | bytes 1081352 | tf_op jit(solution)/shard_map/ppermute | solution.py:34
  38.2 10.0 %collective-permute-start.11 = (bf16[352,512]{1,0:T(8,128)(2,1)S(1)}, bf16[352,512]{1,0:T(8,128)(2,1)}, u32[]{:S(2)}, u32[]{:S(2)}) collective-permute-start(bf16[352,512]{1,0:T(8,128)(2,1)S(1)} %pad_maximum_fusion.2.refs_0_), channel_id=1, source_target_pairs={{0,48},{16,32},{32,16},{48,0},{1,49},{17,33},{33,17},{49,1},{2,50}... | collective-permute-start | bytes 1081352 | tf_op jit(solution)/shard_map/ppermute | solution.py:34
  52.3 15.1 %collective-permute-start.12 = (bf16[256,1024]{1,0:T(8,128)(2,1)S(1)}, bf16[256,1024]{1,0:T(8,128)(2,1)}, u32[]{:S(2)}, u32[]{:S(2)}) collective-permute-start(bf16[256,1024]{1,0:T(8,128)(2,1)S(1)} %pad_maximum_fusion.pair), channel_id=1, source_target_pairs={{0,4},{2,6},{4,0},{6,2},{1,5},{3,7},{5,1},{7,3},{8,12},{10,14},{12... | collective-permute-start | bytes 1572872 | tf_op jit(solution)/shard_map/ppermute | solution.py:34
  54.9 14.1 %collective-permute-start.17 = (bf16[352,512]{1,0:T(8,128)(2,1)S(1)}, bf16[352,512]{1,0:T(8,128)(2,1)}, u32[]{:S(2)}, u32[]{:S(2)}) collective-permute-start(bf16[352,512]{1,0:T(8,128)(2,1)S(1)} %pad_maximum_fusion.2.refs_0_), channel_id=1, source_target_pairs={{0,32},{16,48},{32,0},{48,16},{1,33},{17,49},{33,1},{49,17},{2,34}... | collective-permute-start | bytes 1081352 | tf_op jit(solution)/shard_map/ppermute | solution.py:34
  87.0 13.7 %all-to-all-start = ((f32[16,8,128]{2,1,0:T(8,128)}), f32[16,8,128]{2,1,0:T(8,128)S(1)}, u32[]{:S(2)}, u32[]{:S(2)}) async-start(f32[16,8,128]{2,1,0:T(8,128)} %tile.9), calls=%async_computation | async-start | bytes 131072 | tf_op jit(solution)/shard_map/all_to_all | solution.py:251
  110.8 12.8 %collective-permute-start.22 = (bf16[352,2048]{1,0:T(8,128)(2,1)S(1)}, bf16[352,2048]{1,0:T(8,128)(2,1)S(1)}, u32[]{:S(2)}, u32[]{:S(2)}) collective-permute-start(bf16[352,2048]{1,0:T(8,128)(2,1)S(1)} %get-tuple-element.62), channel_id=1, source_target_pairs={{0,8},{8,0},{1,9},{9,1},{2,10},{10,2},{3,11},{11,3},{4,12},{12,4},... | collective-permute-start | bytes 4325384 | tf_op jit(solution)/shard_map/ppermute | solution.py:34
  125.0 10.4 %collective-permute-start.25 = (bf16[352,512]{1,0:T(8,128)(2,1)}, bf16[352,512]{1,0:T(8,128)(2,1)S(1)}, u32[]{:S(2)}, u32[]{:S(2)}) collective-permute-start(bf16[352,512]{1,0:T(8,128)(2,1)} %get-tuple-element.89), channel_id=1, source_target_pairs={{0,16},{16,0},{32,48},{48,32},{1,17},{17,1},{33,49},{49,33},{2,18}... | collective-permute-start | bytes 1081352 | tf_op jit(solution)/shard_map/ppermute | solution.py:34
  125.5 19.3 %collective-permute-start.23 = (bf16[352,512]{1,0:T(8,128)(2,1)}, bf16[352,512]{1,0:T(8,128)(2,1)}, u32[]{:S(2)}, u32[]{:S(2)}) collective-permute-start(bf16[352,512]{1,0:T(8,128)(2,1)} %get-tuple-element.87), channel_id=1, source_target_pairs={{0,32},{16,48},{32,0},{48,16},{1,33},{17,49},{33,1},{49,17},{2,34}... | collective-permute-start | bytes 1081352 | tf_op jit(solution)/shard_map/ppermute | solution.py:34
  128.1 18.7 %collective-permute-start.26 = (bf16[352,512]{1,0:T(8,128)(2,1)}, bf16[352,512]{1,0:T(8,128)(2,1)}, u32[]{:S(2)}, u32[]{:S(2)}) collective-permute-start(bf16[352,512]{1,0:T(8,128)(2,1)} %get-tuple-element.88), channel_id=1, source_target_pairs={{0,48},{16,32},{32,16},{48,0},{1,49},{17,33},{33,17},{49,1},{2,50}... | collective-permute-start | bytes 1081352 | tf_op jit(solution)/shard_map/ppermute | solution.py:34
  131.3 26.1 %collective-permute-start.27 = (bf16[352,512]{1,0:T(8,128)(2,1)}, bf16[352,512]{1,0:T(8,128)(2,1)}, u32[]{:S(2)}, u32[]{:S(2)}) collective-permute-start(bf16[352,512]{1,0:T(8,128)(2,1)} %get-tuple-element.85), channel_id=1, source_target_pairs={{0,16},{16,0},{32,48},{48,32},{1,17},{17,1},{33,49},{49,33},{2,18}... | collective-permute-start | bytes 1081352 | tf_op jit(solution)/shard_map/ppermute | solution.py:34
  131.3 30.9 %collective-permute-start.28 = (bf16[352,512]{1,0:T(8,128)(2,1)}, bf16[352,512]{1,0:T(8,128)(2,1)}, u32[]{:S(2)}, u32[]{:S(2)}) collective-permute-start(bf16[352,512]{1,0:T(8,128)(2,1)} %get-tuple-element.84), channel_id=1, source_target_pairs={{0,48},{16,32},{32,16},{48,0},{1,49},{17,33},{33,17},{49,1},{2,50}... | collective-permute-start | bytes 1081352 | tf_op jit(solution)/shard_map/ppermute | solution.py:34
  148.5 18.2 %collective-permute-start.29 = (bf16[352,512]{1,0:T(8,128)(2,1)}, bf16[352,512]{1,0:T(8,128)(2,1)S(1)}, u32[]{:S(2)}, u32[]{:S(2)}) collective-permute-start(bf16[352,512]{1,0:T(8,128)(2,1)} %get-tuple-element.68), channel_id=1, source_target_pairs={{0,32},{16,48},{32,0},{48,16},{1,33},{17,49},{33,1},{49,17},{2,34}... | collective-permute-start | bytes 1081352 | tf_op jit(solution)/shard_map/ppermute | solution.py:34
  150.2 12.0 %collective-permute-start.30 = (bf16[368,128]{1,0:T(8,128)(2,1)}, bf16[368,128]{1,0:T(8,128)(2,1)S(1)}, u32[]{:S(2)}, u32[]{:S(2)}) collective-permute-start(bf16[368,128]{1,0:T(8,128)(2,1)} %get-tuple-element.69), channel_id=1, source_target_pairs={{0,128},{128,0},{1,129},{129,1},{2,130},{130,2},{3,131},{131,3},{4... | collective-permute-start | bytes 282632 | tf_op jit(solution)/shard_map/ppermute | solution.py:34
  156.9 9.7 %collective-permute-start.31 = (bf16[368,128]{1,0:T(8,128)(2,1)}, bf16[368,128]{1,0:T(8,128)(2,1)S(1)}, u32[]{:S(2)}, u32[]{:S(2)}) collective-permute-start(bf16[368,128]{1,0:T(8,128)(2,1)} %get-tuple-element.70), channel_id=1, source_target_pairs={{0,64},{64,0},{1,65},{65,1},{2,66},{66,2},{3,67},{67,3},{4,68},{68... | collective-permute-start | bytes 282632 | tf_op jit(solution)/shard_map/ppermute | solution.py:34
  168.4 13.2 %collective-permute-start.32 = (bf16[736,128]{1,0:T(8,128)(2,1)S(1)}, bf16[736,128]{1,0:T(8,128)(2,1)S(1)}, u32[]{:S(2)}, u32[]{:S(2)}) collective-permute-start(bf16[736,128]{1,0:T(8,128)(2,1)S(1)} %pad_maximum_fusion.3), channel_id=1, source_target_pairs={{0,192},{64,128},{128,64},{192,0},{1,193},{65,129},{129,65},{193,1... | collective-permute-start | bytes 565256 | tf_op jit(solution)/shard_map/ppermute | solution.py:34
  169.2 11.7 %collective-permute-start.34 = (bf16[368,128]{1,0:T(8,128)(2,1)S(1)}, bf16[368,128]{1,0:T(8,128)(2,1)S(1)}, u32[]{:S(2)}, u32[]{:S(2)}) collective-permute-start(bf16[368,128]{1,0:T(8,128)(2,1)S(1)} %get-tuple-element.79), channel_id=1, source_target_pairs={{0,64},{64,0},{1,65},{65,1},{2,66},{66,2},{3,67},{67,3},{4,68},{68... | collective-permute-start | bytes 282632 | tf_op jit(solution)/shard_map/ppermute | solution.py:34
  171.1 9.8 %collective-permute-start.33 = (bf16[368,128]{1,0:T(8,128)(2,1)S(1)}, bf16[368,128]{1,0:T(8,128)(2,1)S(1)}, u32[]{:S(2)}, u32[]{:S(2)}) collective-permute-start(bf16[368,128]{1,0:T(8,128)(2,1)S(1)} %get-tuple-element.78), channel_id=1, source_target_pairs={{0,128},{128,0},{1,129},{129,1},{2,130},{130,2},{3,131},{131,3},{4... | collective-permute-start | bytes 282632 | tf_op jit(solution)/shard_map/ppermute | solution.py:34
  (26 other events, 180.9 us)
where the time goes:
time: 189 us; the launch traced here: 188 us
  waiting for transfers between devices  59.9 us (32%)
  starting transfers between devices  57.7 us (31%)
  Pallas kernels  42.4 us (22%)
  other arithmetic  13.8 us (7%)
  local copies, waits for them, and re-layouts  13.4 us (7%)
    ppermute x36, waiting for transfers between devices, swap(): return lax.ppermute(value, names, pairs)  53.2 us
    ppermute x36, starting transfers between devices, swap(): return lax.ppermute(value, names, pairs)  51.1 us
    pallas_call x4, Pallas kernels, vmem_call(): pl.pallas_call(body, out_shape=tuple(out_shape), in_specs=[pl.BlockSpec(m...  42.4 us
    all_to_all x1, waiting for transfers between devices, body(): lax.all_to_all(total, ('h', 'x', 'zl'), 0, 0, tiled=True)  6.73 us
    all_to_all x1, starting transfers between devices, body(): lax.all_to_all(total, ('h', 'x', 'zl'), 0, 0, tiled=True)  6.67 us
    unnamed x28, local copies, waits for them, and re-layouts  6.15 us
  transfers between devices with their start and end apart: 37, of which 18 were waited for; matrix products, arithmetic and copies ran while one was open for 6% of the time, Pallas kernels for 11%

commit v1 on v0

v1 whole, which is shorter than its diff:
```python
import jax
import jax.numpy as jnp
from jax import lax
from jax.experimental import pallas as pl
from jax.experimental.pallas import tpu as pltpu
from jax.sharding import Mesh, PartitionSpec as P

SIZE = {"g": 2, "h": 2, "y": 4, "c": 2, "x": 4, "zl": 2}
AXES = tuple(SIZE)
BF = jnp.bfloat16
F32 = jnp.float32
SLAB = 128
ORDER = (0, 1, 3, 2)
PART = 128


def swap(value, zh=0, **masks):
    if zh:
        masks = dict(masks, g=zh // 2, h=zh % 2)
    masks = {a: m for a, m in masks.items() if m}
    names = tuple(a for a in AXES if a in masks)
    pairs, count = [], 1
    for a in names:
        count *= SIZE[a]
    for i in range(count):
        left, at = i, {}
        for a in reversed(names):
            at[a] = left % SIZE[a]
            left //= SIZE[a]
        j = 0
        for a in names:
            j = j * SIZE[a] + (at[a] ^ masks[a])
        pairs.append((i, j))
    return lax.ppermute(value, names, pairs)


def normalized(rows):
    values = rows.astype(F32)
    scale = lax.rsqrt(jnp.mean(values * values, axis=-1, keepdims=True) + 1e-06)
    return (values * scale).astype(BF)


def unit_slabs(at, points, features):
    def body(at, points, features, out, out_rows):
        out[...] = normalized(points[...])
        out_rows[...] = normalized(features[...])

    spec = lambda k: pl.BlockSpec((SLAB, points.shape[1]), lambda i, at: (at[k], 0))
    kept = pl.BlockSpec((SLAB, points.shape[1]), lambda i, at: (0, 0))
    shape = jax.ShapeDtypeStruct((SLAB, points.shape[1]), BF)
    grid = pltpu.PrefetchScalarGridSpec(
        num_scalar_prefetch=1, grid=(1,), in_specs=[spec(0), spec(1)], out_specs=[kept, kept]
    )
    return pl.pallas_call(body, grid_spec=grid, out_shape=[shape, shape], name="unit_slabs")(at, points, features)


def whole(value):
    return pl.BlockSpec(value.shape, lambda i: (0,) * value.ndim, pipeline_mode=pl.Buffered(1))


def stepped(body, name, steps, given, in_specs, out_shape, out_specs, scratch, flops):
    moved = 4 * sum(v.size for v in given)
    return pl.pallas_call(
        body,
        grid=(steps,),
        out_shape=out_shape,
        in_specs=in_specs,
        out_specs=out_specs,
        scratch_shapes=scratch,
        compiler_params=pltpu.CompilerParams(vmem_limit_bytes=48 << 20),
        cost_estimate=pl.CostEstimate(flops=flops, bytes_accessed=moved, transcendentals=0),
        name=name,
    )(*given)


def write_rows(left, table, place, first, factor, out, out_sq):
    dots = lax.dot_general(left, table, (((1,), (1,)), ((), ())), preferred_element_type=F32)
    value = jnp.exp(dots * factor).astype(BF)
    square = value * value
    for kl in range(2):
        to = pl.ds(pl.multiple_of(place[first + kl] * SLAB, SLAB), SLAB)
        out[:, to] = value[:, kl * SLAB : (kl + 1) * SLAB]
        out_sq[:, to] = square[:, kl * SLAB : (kl + 1) * SLAB]


def near_rows(places, features, relay, relay_far, pair, across, packs, across_packs):
    own, width = features.shape
    factor = 1.0 / float(width) ** 0.5
    step = 256

    def body(place, feature, relay, relay_far, pair, across, near, back, near_a, back_a, out, out_sq, rows_out, held):
        i = pl.program_id(0)

        @pl.when(i == 0)
        def _():
            held[pl.ds(pl.multiple_of(place[16] * own, own), own)] = normalized(feature[...])
            for k, rows in enumerate((relay, near, relay_far, back)):
                at = pl.ds(pl.multiple_of(place[12 + k] * PART, PART), PART)
                held[at] = rows[...] if k % 2 == 0 else rows[2 * SLAB :]

        left = held[pl.ds(pl.multiple_of(i * step, step), step)]
        rows_out[...] = left
        for n, table in enumerate((pair, across, near, near_a, back, back_a)):
            write_rows(left, table[: 2 * SLAB], place, 2 * n, factor, out, out_sq)

    given = [places, features, relay, relay_far, pair, across, *packs, *across_packs]
    shapes = [jax.ShapeDtypeStruct((2 * own, n), BF) for n in (12 * SLAB, 12 * SLAB, width)]
    return stepped(
        body,
        "near_rows",
        2 * own // step,
        given,
        [pl.BlockSpec(memory_space=pltpu.SMEM)] + [whole(v) for v in given[1:]],
        shapes,
        [pl.BlockSpec((step, s.shape[1]), lambda i: (i, 0)) for s in shapes],
        [pltpu.VMEM((2 * own, width), BF)],
        4 * own * 12 * SLAB * width,
    )


def means_of(places, rows, far, far_across, near_k, ours, theirs, variance, rate):
    count, width = rows.shape
    quarter = ours[0].shape[0]
    factor = 1.0 / float(width) ** 0.5
    step, cut = 256, 3 * SLAB

    def body(place, rows, far, far_across, near_k, *refs):
        blocks, (variance, rate, out, out_sq, ratio, slope, total, weights, held) = refs[:8], refs[8:]

        @pl.when(pl.program_id(0) == 0)
        def _():
            for k in range(2):
                here = slice(k * quarter, (k + 1) * quarter)
                for ky in range(4):
                    block = blocks[4 * k + ky]
                    weights[here, ky * cut : (ky + 1) * cut] = block[:, :cut]
                    weights[here, 12 * SLAB + ky * SLAB : 12 * SLAB + (ky + 1) * SLAB] = block[:, cut:]

        for n, table in enumerate((far, far_across)):
            write_rows(rows[...], table[...], place, 2 * n, factor, out, out_sq)
        transposed = (((1,), (1,)), ((), ()))
        held[...] = lax.dot_general(
            weights[:, : 12 * SLAB], near_k[...], transposed, preferred_element_type=F32
        ) + lax.dot_general(weights[:, 12 * SLAB :], out[...], transposed, preferred_element_type=F32)
        part = jnp.zeros((1, step), F32)
        for k in range(4):
            here = slice(k * quarter // 2, (k + 1) * quarter // 2)
            means = held[here]
            square = means * means + variance[here]
            inverse = lax.rsqrt(square)
            spread = square * inverse
            small = jnp.exp(-spread)
            share = 1.0 / (1.0 + small)
            value = rate[here] * jnp.exp(-(means + spread) * 0.5) * share
            ratio[here] = value
            slope[here] = (1.0 - small) * share * (0.5 * inverse)
            part += jnp.sum(value, axis=0, keepdims=True)
        total[...] = part

    given = [places, rows, far, far_across, near_k, *ours, *theirs, variance, rate]
    wide = jax.ShapeDtypeStruct((2 * quarter, count), F32)
    last = jax.ShapeDtypeStruct((count, 4 * SLAB), BF)
    by_rows = lambda v: pl.BlockSpec((step, v.shape[1]), lambda i: (i, 0))
    by_columns = lambda v: pl.BlockSpec((v.shape[0], step), lambda i: (0, i))
    total = jax.ShapeDtypeStruct((1, count), F32)
    return stepped(
        body,
        "means",
        count // step,
        given,
        [pl.BlockSpec(memory_space=pltpu.SMEM), by_rows(rows), whole(far), whole(far_across), by_rows(near_k)]
        + [whole(v) for v in given[5:]],
        [pltpu.HBM(last.shape, BF), pltpu.HBM(last.shape, BF), wide, wide, total],
        [by_rows(last), by_rows(last), by_columns(wide), by_columns(wide), by_columns(total)],
        [pltpu.VMEM((2 * quarter, 16 * SLAB), BF), pltpu.VMEM((2 * quarter, step), F32)],
        2 * count * 16 * SLAB * 2 * quarter,
    )


def statistic(ratio, slope, intensity, labels, ids, near, last):
    quarter, count = ratio.shape[0] // 2, ratio.shape[1]
    steps = 4

    def body(*refs):
        ratio, slope = refs[0], refs[1] if slopes else None
        intensity, labels, ids, near, last, keep, give, weight, joint = refs[1 + len(slopes) :]

        @pl.when(pl.program_id(0) == 0)
        def _():
            for k in range(4):
                here = slice(k * quarter // 2, (k + 1) * quarter // 2)
                hot = (ids[here] == labels[...]).astype(F32)
                expected = intensity[...] * ratio[here]
                value = (hot - expected) * 0.5 if slope is None else (hot + expected) * slope[here]
                weight[here] = value.astype(BF)

        joint[:, : 3 * SLAB] = near[...]
        joint[:, 3 * SLAB :] = last[...]
        sums = jnp.dot(weight[...], joint[...], preferred_element_type=F32)
        keep[...] = sums[:quarter]
        give[...] = sums[quarter:].astype(BF)

    slopes = [] if slope is None else [slope]
    given = [ratio, *slopes, intensity, labels, ids, near, last]
    block = lambda rows, cols: pl.BlockSpec((rows, cols), lambda i: (0, i))
    return stepped(
        body,
        "statistic",
        steps,
        given,
        [whole(v) for v in given[:-2]] + [block(count, 3 * SLAB), block(count, SLAB)],
        [jax.ShapeDtypeStruct((quarter, 16 * SLAB), F32), jax.ShapeDtypeStruct((quarter, 16 * SLAB), BF)],
        [block(quarter, 4 * SLAB), block(quarter, 4 * SLAB)],
        [pltpu.VMEM(ratio.shape, BF), pltpu.VMEM((count, 4 * SLAB), BF)],
        2 * count * 16 * SLAB * 2 * quarter,
    )


def body(features, labels, inducing, mean_weights, class_variance, class_rate):
    g, h, y, c, x, zl = (lax.axis_index(a) for a in AXES)
    zh = 2 * g + h
    all_local = mean_weights.shape[1]
    half = all_local // 2
    quarter = half // 2

    mine, relay = unit_slabs(jnp.stack([c, x]).astype(jnp.int32), inducing, features)
    mine, relay, mean_weights = lax.optimization_barrier((mine, relay, mean_weights))
    relay = swap(relay, zh=1)
    labs = swap(labels, zh=1)
    pair = jnp.concatenate([mine, swap(mine, zl=1)], 0)

    local = mean_weights.T.reshape(2, 2, quarter, -1)
    keep = lax.dynamic_index_in_dim(local, c, 1, False)
    give = lax.dynamic_index_in_dim(local, 1 - c, 1, False)
    got = swap(give, c=1)
    block = jnp.where(c == 0, jnp.concatenate([keep, got], 2), jnp.concatenate([got, keep], 2))
    same = lax.dynamic_index_in_dim(block, h, 0, False)
    other = lax.dynamic_index_in_dim(block, 1 - h, 0, False)
    over_z = jnp.stack([same, swap(other, zh=1), swap(same, zh=2), swap(other, zh=3)])
    over_z = jnp.concatenate([lax.dynamic_index_in_dim(over_z, zh ^ x ^ kx, 0, False) for kx in ORDER], 1)

    pack = jnp.concatenate([pair, relay], 0)
    near, back = swap(pack, x=1), swap(pack, x=3)
    over_z, pack = lax.optimization_barrier((over_z, pack))
    over_y = [over_z, swap(over_z, y=1), None, swap(over_z, y=3)]
    relay_far, near, back, pair, labs, over_z, over_y[1], over_y[3] = lax.optimization_barrier(
        (swap(relay, x=2), near, back, pair, labs, over_z, over_y[1], over_y[3])
    )
    over_y[2] = swap(over_z, y=2)
    far = swap(pair, x=2)

    def places(order):
        found = []
        for i, kx in enumerate(order):
            for core in (c, 1 - c):
                for kl in range(2):
                    found.append((y ^ ((zl ^ kl) * 2 + core)) * len(order) + i)
        return found

    where = places(ORDER[:3]) + [(1 - h) * 4 + (x ^ kx) for kx in range(4)] + [h]
    where = jnp.stack(where).astype(jnp.int32)
    across = (swap(near, c=1), swap(back, c=1))
    near_k, near_sq, rows = near_rows(where, features, relay, relay_far, pair, swap(pair, c=1), (near, back), across)
    far, rows = lax.optimization_barrier((far, rows))

    def of_classes(value):
        value = lax.dynamic_slice_in_dim(value, h * half, half, 0)
        return jnp.where(c == 0, value, jnp.concatenate([value[quarter:], value[:quarter]]))[:, None]

    ids = (x * 2 + zl) * all_local + of_classes(jnp.arange(all_local, dtype=jnp.int32))
    labs = jnp.where(h == 0, jnp.concatenate([labels, labs]), jnp.concatenate([labs, labels]))[None, :]
    where = jnp.stack(places(ORDER[3:])).astype(jnp.int32)
    last_k, last_sq, ratio, slope, total = means_of(
        where, rows, far, swap(far, c=1), near_k, over_y, [swap(v, c=1) for v in over_y],
        of_classes(class_variance), of_classes(class_rate),
    )
    total = jnp.tile(total.reshape(1, 8, 128), (16, 1, 1))
    total = jnp.sum(lax.all_to_all(total, ("h", "x", "zl"), 0, 0, tiled=True), axis=0).reshape(1, -1)
    all_classes = all_local * 8
    intensity = (1.0 + total) / (1.0 + 0.5 * all_classes)

    def chunks(kept, came):
        parts = [slice(ky * 512, (ky + 1) * 512) for ky in range(4)]
        return [kept[:, at] + came[:, at].astype(F32) for at in parts]

    def over_y_rows(mine, came):
        near, back, far = (value.astype(F32) for value in came)
        return (mine + far) + (near + back)

    def slab_of(value, kz):
        kx = x ^ zh ^ kz
        return lax.dynamic_slice_in_dim(value, (kx ^ (kx // 2)) * SLAB, SLAB, 1)

    def outgoing(own):
        middle = lax.reduce_precision(jnp.mean(own, axis=1), 8, 7)
        rest = (own - middle[:, None]).astype(BF)
        tail = jnp.pad(middle.astype(BF), (0, 16 * SLAB - quarter)).reshape(16, SLAB)
        return [jnp.concatenate([slab_of(rest, kz), tail], 0) for kz in (2, 1, 3)]

    def incoming(value):
        middle = value[quarter:].reshape(-1)[:quarter]
        return value[:quarter].astype(F32) + middle.astype(F32)[:, None]

    def total_of(own, got):
        got = [incoming(value) for value in got]
        return jnp.stack([slab_of(own, 0) + got[0], got[1] + got[2]])

    kept, give = statistic(ratio, None, intensity, labs, ids, near_k, last_k)
    first = chunks(kept, swap(give, c=1))
    sent = [first[ky].astype(BF) for ky in (1, 3, 2)]
    came = [swap(value, y=ky) for value, ky in zip(sent, (1, 3, 2))]
    kept, give = statistic(ratio, slope, intensity, labs, ids, near_sq, last_sq)
    second = chunks(kept, swap(give, c=1))
    rest = [swap(second[ky].astype(BF), y=ky) for ky in (1, 3)]
    far, came[0] = lax.optimization_barrier((second[2].astype(BF), came[0]))
    rest.append(swap(far, y=2))

    first = over_y_rows(first[0], came)
    send = lax.optimization_barrier(outgoing(first))
    got = [swap(send[0], zh=2), swap(send[1], zh=1)]
    rest, got = lax.optimization_barrier((rest, got))
    late = send[2]
    second = over_y_rows(second[0], rest)
    send = lax.optimization_barrier(outgoing(second))
    both = swap(jnp.concatenate([send[2], late], 0), zh=3)
    first = total_of(first, got + [both[quarter + 16 :]])
    second = total_of(second, [swap(send[0], zh=2), swap(send[1], zh=1), both[: quarter + 16]])
    summed = jnp.stack([first, second]).transpose(0, 3, 1, 2) * (1.0 / (512 * 32))
    mine = lax.dynamic_slice_in_dim(summed, c * 64, 64, 1)
    theirs = swap(lax.dynamic_slice_in_dim(summed, (1 - c) * 64, 64, 1), c=1)

    def in_order(mine, theirs):
        pieces = []
        for half in range(2):
            same, other = (jnp.where(h == half, v[:, 0], v[:, 1]) for v in (mine, theirs))
            pieces += [jnp.where(c == 0, same, other), jnp.where(c == 0, other, same)]
        return jnp.concatenate(pieces, 1)

    return in_order(mine[0], theirs[0]), in_order(mine[1], theirs[1])


def solution(mesh):
    parts = Mesh(mesh.devices.reshape(tuple(SIZE.values())), AXES)
    dp, cls = ("g", "h", "y", "c"), ("x", "zl")
    in_specs = (P(dp, None), P(dp), P(cls, None), P(dp, cls), P(cls), P(cls))
    out_specs = (P(dp, cls), P(dp, cls))
    return jax.shard_map(body, mesh=parts, in_specs=in_specs, out_specs=out_specs, check_vma=False)
```

time: 189 us -> 183 us (0.968)
  Pallas kernels: 42.4 us -> 37.9 us
  waiting for transfers between devices: 59.9 us -> 62.7 us
  other arithmetic: 13.8 us -> 11.1 us
    pallas_call x4 -> x5, Pallas kernels: 42.4 us -> 37.9 us  [the longest x4 35.3 us: stepped(): pl.pallas_call(body, grid=(steps,), out_shape=out_shape, in_specs=in_spec...]
    ppermute x36, waiting for transfers between devices: 53.2 us -> 55.9 us  [swap(): return lax.ppermute(value, names, pairs)]
    reduce_sum x2 -> x0, other arithmetic: 2.21 us -> none  [normalized(): scale = lax.rsqrt(jnp.mean(values * values, axis=-1, keepdims=True) + 1e-06)]
    unnamed x28 -> x30, local copies, waits for them, and re-layouts: 6.15 us -> 8.36 us
    squeeze x2 -> x1, local copies, waits for them, and re-layouts: 2.1 us -> 0.05 us  [body(): return (in_order(mine[0], theirs[0]), in_order(mine[1], theirs[1]))]
    convert_element_type x3 -> x2, other arithmetic: 5.03 us -> 3.91 us  [the longest x1 2.46 us: body(): rest = [swap(second[ky].astype(BF), y=ky) for ky in (1, 3)]]
  transfers between devices with their start and end apart: 37 -> 37, of which waited for: 18 -> 20; matrix products, arithmetic and copies ran while one was open for 6% -> 7% of each run, Pallas kernels for 11% -> 10%
where the time goes in v1:
time: 183 us; the launch traced here: 182 us
  waiting for transfers between devices  62.7 us (34%)
  starting transfers between devices  56 us (31%)
  Pallas kernels  37.9 us (21%)
  local copies, waits for them, and re-layouts  13.6 us (7%)
  other arithmetic  11.1 us (6%)
    ppermute x36, waiting for transfers between devices, swap(): return lax.ppermute(value, names, pairs)  55.9 us
    ppermute x36, starting transfers between devices, swap(): return lax.ppermute(value, names, pairs)  50.4 us
    pallas_call x4, Pallas kernels, stepped(): pl.pallas_call(body, grid=(steps,), out_shape=out_shape, in_specs=in_spec...  35.3 us
    unnamed x30, local copies, waits for them, and re-layouts  8.36 us
    all_to_all x1, waiting for transfers between devices, body(): lax.all_to_all(total, ('h', 'x', 'zl'), 0, 0, tiled=True)  6.83 us
    all_to_all x1, starting transfers between devices, body(): lax.all_to_all(total, ('h', 'x', 'zl'), 0, 0, tiled=True)  5.59 us
  transfers between devices with their start and end apart: 37, of which 20 were waited for; matrix products, arithmetic and copies ran while one was open for 7% of the time, Pallas kernels for 10%

profile of v1, /device:TPU:1, one launch (start us, length us, event | category | flops | bytes accessed | tf_op | source)
XLA Modules:
  0.0 182.4 jit_solution(16018015447981761096)
XLA Ops:
  1.2 2.6 %unit_slabs.1 = (bf16[128,1024]{1,0:T(8,128)(2,1)}, bf16[128,1024]{1,0:T(8,128)(2,1)}) custom-call(s32[2]{0:T(128)} %pad_add_fusion.1.at, bf16[256,1024]{1,0:T(8,128)(2,1)} %points.1, bf16[512,1024]{1,0:T(8,128)(2,1)} %feature.1), custom_call_target="tpu_custom_call" | custom-call | tf_op jit(solution)/shard_map/unit_slabs/pallas_call | solution.py:54
  5.7 3.3 %collective-permute-start.6 = (bf16[2,352,64]{2,1,0:T(8,128)(2,1)S(1)}, bf16[2,352,64]{2,1,0:T(8,128)(2,1)S(1)}, u32[]{:S(2)}, u32[]{:S(2)}) collective-permute-start(bf16[2,352,64]{2,1,0:T(8,128)(2,1)S(1)} %bitcast.108), channel_id=1, source_target_pairs={{0,8},{8,0},{1,9},{9,1},{2,10},{10,2},{3,11},{11,3},{4,12},{12,4},... | collective-permute-start | bytes 270344 | tf_op jit(solution)/shard_map/ppermute | solution.py:34
  9.0 2.9 %collective-permute-start = (bf16[128,1024]{1,0:T(8,128)(2,1)}, bf16[128,1024]{1,0:T(8,128)(2,1)S(1)}, u32[]{:S(2)}, u32[]{:S(2)}) collective-permute-start(bf16[128,1024]{1,0:T(8,128)(2,1)} %get-tuple-element.45), channel_id=1, source_target_pairs={{0,64},{64,0},{1,65},{65,1},{2,66},{66,2},{3,67},{67,3},{4,68},{68... | collective-permute-start | bytes 786440 | tf_op jit(solution)/shard_map/ppermute | solution.py:34
  14.2 4.5 %collective-permute-start.9 = (bf16[352,128]{1,0:T(8,128)(2,1)S(1)}, bf16[352,128]{1,0:T(8,128)(2,1)S(1)}, u32[]{:S(2)}, u32[]{:S(2)}) collective-permute-start(bf16[352,128]{1,0:T(8,128)(2,1)S(1)} %get-tuple-element.133), channel_id=1, source_target_pairs={{0,192},{64,128},{128,64},{192,0},{1,193},{65,129},{129,65},{193,1... | collective-permute-start | bytes 270344 | tf_op jit(solution)/shard_map/ppermute | solution.py:34
  19.8 4.6 %collective-permute-done.2 = bf16[128,1024]{1,0:T(8,128)(2,1)S(1)} collective-permute-done((bf16[128,1024]{1,0:T(8,128)(2,1)}, bf16[128,1024]{1,0:T(8,128)(2,1)S(1)}, u32[]{:S(2)}, u32[]{:S(2)}) %collective-permute-start.2) | collective-permute-done | bytes 262176 | tf_op jit(solution)/shard_map/ppermute | solution.py:34
  26.3 7.8 %collective-permute-done.8 = bf16[352,128]{1,0:T(8,128)(2,1)S(1)} collective-permute-done((bf16[352,128]{1,0:T(8,128)(2,1)S(1)}, bf16[352,128]{1,0:T(8,128)(2,1)S(1)}, u32[]{:S(2)}, u32[]{:S(2)}) %collective-permute-start.8) | collective-permute-done | bytes 90144 | tf_op jit(solution)/shard_map/ppermute | solution.py:34
  37.5 3.7 %collective-permute-done.5 = s32[512]{0:T(512)S(1)} collective-permute-done((s32[512]{0:T(512)S(1)}, s32[512]{0:T(512)S(1)}, u32[]{:S(2)}, u32[]{:S(2)}) %collective-permute-start.5) | collective-permute-done | bytes 2080 | tf_op jit(solution)/shard_map/ppermute | solution.py:34
  43.6 4.4 %collective-permute-done.1.relay_far = bf16[128,1024]{1,0:T(8,128)(2,1)S(1)} collective-permute-done((bf16[128,1024]{1,0:T(8,128)(2,1)S(1)}, bf16[128,1024]{1,0:T(8,128)(2,1)S(1)}, u32[]{:S(2)}, u32[]{:S(2)}) %collective-permute-start.1) | collective-permute-done | bytes 262176 | tf_op jit(solution)/shard_map/ppermute | solution.py:34
  48.8 4.2 %collective-permute-start.14 = (bf16[384,1024]{1,0:T(8,128)(2,1)S(1)}, bf16[384,1024]{1,0:T(8,128)(2,1)}, u32[]{:S(2)}, u32[]{:S(2)}) collective-permute-start(bf16[384,1024]{1,0:T(8,128)(2,1)S(1)} %collective-permute-done.3.near), channel_id=1, source_target_pairs={{0,8},{8,0},{1,9},{9,1},{2,10},{10,2},{3,11},{11,3},{4,12},{12,4},... | collective-permute-start | bytes 2359304 | tf_op jit(solution)/shard_map/ppermute | solution.py:34
  57.9 8.7 %near_rows.1 = (bf16[1024,1536]{1,0:T(8,128)(2,1)}, bf16[1024,1536]{1,0:T(8,128)(2,1)}, bf16[1024,1024]{1,0:T(8,128)(2,1)}) custom-call(s32[17]{0:T(128)S(1)} %stack.147.place, bf16[512,1024]{1,0:T(8,128)(2,1)S(1)} %copy-done.1, bf16[128,1024]{1,0:T(8,128)(2,1)S(1)} %collective-permute-done.relay, bf16[128,1024]{1,0:T(8,128)(2,1)S(1)} %copy-done.3, ...), custom_call_target="tpu_custom_call" | custom-call | flops 3221225472 | bytes 11534404 | tf_op jit(solution)/shard_map/near_rows/pallas_call | solution.py:63
  73.6 10.9 %means.1 = (bf16[1024,512]{1,0:T(8,128)(2,1)}, bf16[1024,512]{1,0:T(8,128)(2,1)}, f32[704,1024]{1,0:T(8,128)}, f32[704,1024]{1,0:T(8,128)}, f32[1,1024]{1,0:T(1,128)S(1)}) custom-call(s32[4]{0:T(128)S(1)} %pad_add_fusion.place, bf16[1024,1024]{1,0:T(8,128)(2,1)} %get-tuple-element.54.rows, bf16[256,1024]{1,0:T(8,128)(2,1)} %collective-permute-done.12.far, ...), custom_call_target="tpu_custom_call" | custom-call | flops 2952790016 | bytes 18355728 | tf_op jit(solution)/shard_map/means/pallas_call | solution.py:63
  85.2 5.6 %all-to-all-start = ((f32[16,8,128]{2,1,0:T(8,128)}), f32[16,8,128]{2,1,0:T(8,128)S(1)}, u32[]{:S(2)}, u32[]{:S(2)}) async-start(f32[16,8,128]{2,1,0:T(8,128)} %tile.9), calls=%async_computation | async-start | bytes 131072 | tf_op jit(solution)/shard_map/all_to_all | solution.py:278
  91.0 6.8 %all-to-all-done = f32[16,8,128]{2,1,0:T(8,128)S(1)} async-done(((f32[16,8,128]{2,1,0:T(8,128)}), f32[16,8,128]{2,1,0:T(8,128)S(1)}, u32[]{:S(2)}, u32[]{:S(2)}) %all-to-all-start) | async-done | bytes 65568 | tf_op jit(solution)/shard_map/all_to_all | solution.py:278
  99.1 7.0 %statistic.2 = (f32[352,2048]{1,0:T(8,128)S(1)}, bf16[352,2048]{1,0:T(8,128)(2,1)S(1)}) custom-call(f32[704,1024]{1,0:T(8,128)} %get-tuple-element.60.refs_0_, f32[1,1024]{1,0:T(1,128)S(1)} %bitcast.101, s32[1,1024]{1,0:T(1,128)S(1)} %broadcast_select_fusion.refs_2_.refs_3_, s32[704,1]{1,0:T(8,128)S(1)} %add.323.refs_3_.refs_4_, ...), custom_call_target="tpu_custom_call" | custom-call | flops 2952790016 | bytes 11283200 | tf_op jit(solution)/shard_map/statistic/pallas_call | solution.py:63
  107.9 8.7 %statistic.3 = (f32[352,2048]{1,0:T(8,128)S(1)}, bf16[352,2048]{1,0:T(8,128)(2,1)}) custom-call(f32[704,1024]{1,0:T(8,128)} %get-tuple-element.60.refs_0_, f32[704,1024]{1,0:T(8,128)} %get-tuple-element.66.refs_1_, f32[1,1024]{1,0:T(1,128)S(1)} %bitcast.102, s32[1,1024]{1,0:T(1,128)S(1)} %broadcast_select_fusion.refs_2_.refs_3_, ...), custom_call_target="tpu_custom_call" | custom-call | flops 2952790016 | bytes 14166784 | tf_op jit(solution)/shard_map/statistic/pallas_call | solution.py:63
  120.0 2.6 %collective-permute-start.23 = (bf16[352,512]{1,0:T(8,128)(2,1)}, bf16[352,512]{1,0:T(8,128)(2,1)}, u32[]{:S(2)}, u32[]{:S(2)}) collective-permute-start(bf16[352,512]{1,0:T(8,128)(2,1)} %get-tuple-element.99), channel_id=1, source_target_pairs={{0,32},{16,48},{32,0},{48,16},{1,33},{17,49},{33,1},{49,17},{2,34}... | collective-permute-start | bytes 1081352 | tf_op jit(solution)/shard_map/ppermute | solution.py:34
  122.9 2.5 %add_convert_fusion = (bf16[352,512]{1,0:T(8,128)(2,1)}, bf16[352,512]{1,0:T(8,128)(2,1)}, bf16[352,512]{1,0:T(8,128)(2,1)}) fusion(f32[352,2048]{1,0:T(8,128)S(1)} %get-tuple-element.69, bf16[352,2048]{1,0:T(8,128)(2,1)} %collective-permute-done.24), kind=kLoop, calls=%fused_computation.8 | loop fusion | flops 1622016 | bytes 4325376 | tf_op jit(solution)/shard_map/convert_element_type | solution.py:314
  125.3 2.4 %collective-permute-start.28 = (bf16[352,512]{1,0:T(8,128)(2,1)}, bf16[352,512]{1,0:T(8,128)(2,1)}, u32[]{:S(2)}, u32[]{:S(2)}) collective-permute-start(bf16[352,512]{1,0:T(8,128)(2,1)} %get-tuple-element.96), channel_id=1, source_target_pairs={{0,48},{16,32},{32,16},{48,0},{1,49},{17,33},{33,17},{49,1},{2,50}... | collective-permute-start | bytes 1081352 | tf_op jit(solution)/shard_map/ppermute | solution.py:34
  129.4 9.9 %collective-permute-done.23 = bf16[352,512]{1,0:T(8,128)(2,1)} collective-permute-done((bf16[352,512]{1,0:T(8,128)(2,1)}, bf16[352,512]{1,0:T(8,128)(2,1)}, u32[]{:S(2)}, u32[]{:S(2)}) %collective-permute-start.23) | collective-permute-done | bytes 360480 | tf_op jit(solution)/shard_map/ppermute | solution.py:34
  144.8 6.7 %collective-permute-start.30 = (bf16[368,128]{1,0:T(8,128)(2,1)}, bf16[368,128]{1,0:T(8,128)(2,1)S(1)}, u32[]{:S(2)}, u32[]{:S(2)}) collective-permute-start(bf16[368,128]{1,0:T(8,128)(2,1)} %get-tuple-element.73), channel_id=1, source_target_pairs={{0,128},{128,0},{1,129},{129,1},{2,130},{130,2},{3,131},{131,3},{4... | collective-permute-start | bytes 282632 | tf_op jit(solution)/shard_map/ppermute | solution.py:34
  152.0 4.8 %collective-permute-done.28 = bf16[352,512]{1,0:T(8,128)(2,1)} collective-permute-done((bf16[352,512]{1,0:T(8,128)(2,1)}, bf16[352,512]{1,0:T(8,128)(2,1)}, u32[]{:S(2)}, u32[]{:S(2)}) %collective-permute-start.28) | collective-permute-done | bytes 360480 | tf_op jit(solution)/shard_map/ppermute | solution.py:34
  156.7 4.5 %collective-permute-done.31 = bf16[368,128]{1,0:T(8,128)(2,1)S(1)} collective-permute-done((bf16[368,128]{1,0:T(8,128)(2,1)}, bf16[368,128]{1,0:T(8,128)(2,1)S(1)}, u32[]{:S(2)}, u32[]{:S(2)}) %collective-permute-start.31) | collective-permute-done | bytes 94240 | tf_op jit(solution)/shard_map/ppermute | solution.py:34
  165.6 3.1 %collective-permute-start.33 = (bf16[368,128]{1,0:T(8,128)(2,1)S(1)}, bf16[368,128]{1,0:T(8,128)(2,1)S(1)}, u32[]{:S(2)}, u32[]{:S(2)}) collective-permute-start(bf16[368,128]{1,0:T(8,128)(2,1)S(1)} %get-tuple-element.82), channel_id=1, source_target_pairs={{0,128},{128,0},{1,129},{129,1},{2,130},{130,2},{3,131},{131,3},{4... | collective-permute-start | bytes 282632 | tf_op jit(solution)/shard_map/ppermute | solution.py:34
  169.8 5.7 %collective-permute-done.33 = bf16[368,128]{1,0:T(8,128)(2,1)S(1)} collective-permute-done((bf16[368,128]{1,0:T(8,128)(2,1)S(1)}, bf16[368,128]{1,0:T(8,128)(2,1)S(1)}, u32[]{:S(2)}, u32[]{:S(2)}) %collective-permute-start.33) | collective-permute-done | bytes 94240 | tf_op jit(solution)/shard_map/ppermute | solution.py:34
  (154 shorter events, 53.4 us)
Async XLA Ops:
  9.0 15.4 %collective-permute-start.2 = (bf16[128,1024]{1,0:T(8,128)(2,1)}, bf16[128,1024]{1,0:T(8,128)(2,1)S(1)}, u32[]{:S(2)}, u32[]{:S(2)}) collective-permute-start(bf16[128,1024]{1,0:T(8,128)(2,1)} %get-tuple-element.46), channel_id=1, source_target_pairs={{0,1},{1,0},{2,3},{3,2},{4,5},{5,4},{6,7},{7,6},{8,9},{9,8},{10,11... | collective-permute-start | bytes 786440 | tf_op jit(solution)/shard_map/ppermute | solution.py:34
  9.0 16.1 %collective-permute-start = (bf16[128,1024]{1,0:T(8,128)(2,1)}, bf16[128,1024]{1,0:T(8,128)(2,1)S(1)}, u32[]{:S(2)}, u32[]{:S(2)}) collective-permute-start(bf16[128,1024]{1,0:T(8,128)(2,1)} %get-tuple-element.45), channel_id=1, source_target_pairs={{0,64},{64,0},{1,65},{65,1},{2,66},{66,2},{3,67},{67,3},{4,68},{68... | collective-permute-start | bytes 786440 | tf_op jit(solution)/shard_map/ppermute | solution.py:34
  14.1 12.2 %collective-permute-start.7 = (bf16[352,128]{1,0:T(8,128)(2,1)S(1)}, bf16[352,128]{1,0:T(8,128)(2,1)S(1)}, u32[]{:S(2)}, u32[]{:S(2)}) collective-permute-start(bf16[352,128]{1,0:T(8,128)(2,1)S(1)} %get-tuple-element.133), channel_id=1, source_target_pairs={{0,64},{64,0},{1,65},{65,1},{2,66},{66,2},{3,67},{67,3},{4,68},{68... | collective-permute-start | bytes 270344 | tf_op jit(solution)/shard_map/ppermute | solution.py:34
  14.2 19.9 %collective-permute-start.9 = (bf16[352,128]{1,0:T(8,128)(2,1)S(1)}, bf16[352,128]{1,0:T(8,128)(2,1)S(1)}, u32[]{:S(2)}, u32[]{:S(2)}) collective-permute-start(bf16[352,128]{1,0:T(8,128)(2,1)S(1)} %get-tuple-element.133), channel_id=1, source_target_pairs={{0,192},{64,128},{128,64},{192,0},{1,193},{65,129},{129,65},{193,1... | collective-permute-start | bytes 270344 | tf_op jit(solution)/shard_map/ppermute | solution.py:34
  18.7 15.4 %collective-permute-start.8 = (bf16[352,128]{1,0:T(8,128)(2,1)S(1)}, bf16[352,128]{1,0:T(8,128)(2,1)S(1)}, u32[]{:S(2)}, u32[]{:S(2)}) collective-permute-start(bf16[352,128]{1,0:T(8,128)(2,1)S(1)} %bitcast.106), channel_id=1, source_target_pairs={{0,128},{128,0},{1,129},{129,1},{2,130},{130,2},{3,131},{131,3},{4... | collective-permute-start | bytes 270344 | tf_op jit(solution)/shard_map/ppermute | solution.py:34
  25.9 22.9 %collective-permute-start.3 = (bf16[384,1024]{1,0:T(8,128)(2,1)}, bf16[384,1024]{1,0:T(8,128)(2,1)S(1)}, u32[]{:S(2)}, u32[]{:S(2)}) collective-permute-start(bf16[384,1024]{1,0:T(8,128)(2,1)} %constant_dynamic-update-slice_fusion), channel_id=1, source_target_pairs={{0,2},{2,0},{4,6},{6,4},{1,3},{3,1},{5,7},{7,5},{8,10},{10,8},{12,... | collective-permute-start | bytes 2359304 | tf_op jit(solution)/shard_map/ppermute | solution.py:34
  25.9 22.9 %collective-permute-start.4 = (bf16[384,1024]{1,0:T(8,128)(2,1)}, bf16[384,1024]{1,0:T(8,128)(2,1)}, u32[]{:S(2)}, u32[]{:S(2)}) collective-permute-start(bf16[384,1024]{1,0:T(8,128)(2,1)} %constant_dynamic-update-slice_fusion), channel_id=1, source_target_pairs={{0,6},{2,4},{4,2},{6,0},{1,7},{3,5},{5,3},{7,1},{8,14},{10,12},{12... | collective-permute-start | bytes 2359304 | tf_op jit(solution)/shard_map/ppermute | solution.py:34
  34.2 14.6 %collective-permute-start.10 = (bf16[352,512]{1,0:T(8,128)(2,1)S(1)}, bf16[352,512]{1,0:T(8,128)(2,1)}, u32[]{:S(2)}, u32[]{:S(2)}) collective-permute-start(bf16[352,512]{1,0:T(8,128)(2,1)S(1)} %pad_maximum_fusion.4.refs_0_), channel_id=1, source_target_pairs={{0,16},{16,0},{32,48},{48,32},{1,17},{17,1},{33,49},{49,33},{2,18}... | collective-permute-start | bytes 1081352 | tf_op jit(solution)/shard_map/ppermute | solution.py:34
  35.6 13.2 %collective-permute-start.11 = (bf16[352,512]{1,0:T(8,128)(2,1)S(1)}, bf16[352,512]{1,0:T(8,128)(2,1)}, u32[]{:S(2)}, u32[]{:S(2)}) collective-permute-start(bf16[352,512]{1,0:T(8,128)(2,1)S(1)} %pad_maximum_fusion.4.refs_0_), channel_id=1, source_target_pairs={{0,48},{16,32},{32,16},{48,0},{1,49},{17,33},{33,17},{49,1},{2,50}... | collective-permute-start | bytes 1081352 | tf_op jit(solution)/shard_map/ppermute | solution.py:34
  53.8 15.2 %collective-permute-start.12 = (bf16[256,1024]{1,0:T(8,128)(2,1)S(1)}, bf16[256,1024]{1,0:T(8,128)(2,1)}, u32[]{:S(2)}, u32[]{:S(2)}) collective-permute-start(bf16[256,1024]{1,0:T(8,128)(2,1)S(1)} %pad_maximum_fusion.2.pair), channel_id=1, source_target_pairs={{0,4},{2,6},{4,0},{6,2},{1,5},{3,7},{5,1},{7,3},{8,12},{10,14},{12... | collective-permute-start | bytes 1572872 | tf_op jit(solution)/shard_map/ppermute | solution.py:34
  56.0 14.5 %collective-permute-start.17 = (bf16[352,512]{1,0:T(8,128)(2,1)S(1)}, bf16[352,512]{1,0:T(8,128)(2,1)}, u32[]{:S(2)}, u32[]{:S(2)}) collective-permute-start(bf16[352,512]{1,0:T(8,128)(2,1)S(1)} %pad_maximum_fusion.4.refs_0_), channel_id=1, source_target_pairs={{0,32},{16,48},{32,0},{48,16},{1,33},{17,49},{33,1},{49,17},{2,34}... | collective-permute-start | bytes 1081352 | tf_op jit(solution)/shard_map/ppermute | solution.py:34
  85.2 12.7 %all-to-all-start = ((f32[16,8,128]{2,1,0:T(8,128)}), f32[16,8,128]{2,1,0:T(8,128)S(1)}, u32[]{:S(2)}, u32[]{:S(2)}) async-start(f32[16,8,128]{2,1,0:T(8,128)} %tile.9), calls=%async_computation | async-start | bytes 131072 | tf_op jit(solution)/shard_map/all_to_all | solution.py:278
  106.1 11.4 %collective-permute-start.22 = (bf16[352,2048]{1,0:T(8,128)(2,1)S(1)}, bf16[352,2048]{1,0:T(8,128)(2,1)S(1)}, u32[]{:S(2)}, u32[]{:S(2)}) collective-permute-start(bf16[352,2048]{1,0:T(8,128)(2,1)S(1)} %get-tuple-element.65), channel_id=1, source_target_pairs={{0,8},{8,0},{1,9},{9,1},{2,10},{10,2},{3,11},{11,3},{4,12},{12,4},... | collective-permute-start | bytes 4325384 | tf_op jit(solution)/shard_map/ppermute | solution.py:34
  119.0 10.4 %collective-permute-start.25 = (bf16[352,512]{1,0:T(8,128)(2,1)}, bf16[352,512]{1,0:T(8,128)(2,1)S(1)}, u32[]{:S(2)}, u32[]{:S(2)}) collective-permute-start(bf16[352,512]{1,0:T(8,128)(2,1)} %get-tuple-element.101), channel_id=1, source_target_pairs={{0,16},{16,0},{32,48},{48,32},{1,17},{17,1},{33,49},{49,33},{2,18}... | collective-permute-start | bytes 1081352 | tf_op jit(solution)/shard_map/ppermute | solution.py:34
  120.0 19.3 %collective-permute-start.23 = (bf16[352,512]{1,0:T(8,128)(2,1)}, bf16[352,512]{1,0:T(8,128)(2,1)}, u32[]{:S(2)}, u32[]{:S(2)}) collective-permute-start(bf16[352,512]{1,0:T(8,128)(2,1)} %get-tuple-element.99), channel_id=1, source_target_pairs={{0,32},{16,48},{32,0},{48,16},{1,33},{17,49},{33,1},{49,17},{2,34}... | collective-permute-start | bytes 1081352 | tf_op jit(solution)/shard_map/ppermute | solution.py:34
  122.6 18.7 %collective-permute-start.26 = (bf16[352,512]{1,0:T(8,128)(2,1)}, bf16[352,512]{1,0:T(8,128)(2,1)}, u32[]{:S(2)}, u32[]{:S(2)}) collective-permute-start(bf16[352,512]{1,0:T(8,128)(2,1)} %get-tuple-element.100), channel_id=1, source_target_pairs={{0,48},{16,32},{32,16},{48,0},{1,49},{17,33},{33,17},{49,1},{2,50}... | collective-permute-start | bytes 1081352 | tf_op jit(solution)/shard_map/ppermute | solution.py:34
  125.3 26.6 %collective-permute-start.27 = (bf16[352,512]{1,0:T(8,128)(2,1)}, bf16[352,512]{1,0:T(8,128)(2,1)}, u32[]{:S(2)}, u32[]{:S(2)}) collective-permute-start(bf16[352,512]{1,0:T(8,128)(2,1)} %get-tuple-element.97), channel_id=1, source_target_pairs={{0,16},{16,0},{32,48},{48,32},{1,17},{17,1},{33,49},{49,33},{2,18}... | collective-permute-start | bytes 1081352 | tf_op jit(solution)/shard_map/ppermute | solution.py:34
  125.3 31.4 %collective-permute-start.28 = (bf16[352,512]{1,0:T(8,128)(2,1)}, bf16[352,512]{1,0:T(8,128)(2,1)}, u32[]{:S(2)}, u32[]{:S(2)}) collective-permute-start(bf16[352,512]{1,0:T(8,128)(2,1)} %get-tuple-element.96), channel_id=1, source_target_pairs={{0,48},{16,32},{32,16},{48,0},{1,49},{17,33},{33,17},{49,1},{2,50}... | collective-permute-start | bytes 1081352 | tf_op jit(solution)/shard_map/ppermute | solution.py:34
  143.0 18.2 %collective-permute-start.29 = (bf16[352,512]{1,0:T(8,128)(2,1)}, bf16[352,512]{1,0:T(8,128)(2,1)S(1)}, u32[]{:S(2)}, u32[]{:S(2)}) collective-permute-start(bf16[352,512]{1,0:T(8,128)(2,1)} %get-tuple-element.72), channel_id=1, source_target_pairs={{0,32},{16,48},{32,0},{48,16},{1,33},{17,49},{33,1},{49,17},{2,34}... | collective-permute-start | bytes 1081352 | tf_op jit(solution)/shard_map/ppermute | solution.py:34
  144.8 12.0 %collective-permute-start.30 = (bf16[368,128]{1,0:T(8,128)(2,1)}, bf16[368,128]{1,0:T(8,128)(2,1)S(1)}, u32[]{:S(2)}, u32[]{:S(2)}) collective-permute-start(bf16[368,128]{1,0:T(8,128)(2,1)} %get-tuple-element.73), channel_id=1, source_target_pairs={{0,128},{128,0},{1,129},{129,1},{2,130},{130,2},{3,131},{131,3},{4... | collective-permute-start | bytes 282632 | tf_op jit(solution)/shard_map/ppermute | solution.py:34
  151.5 9.7 %collective-permute-start.31 = (bf16[368,128]{1,0:T(8,128)(2,1)}, bf16[368,128]{1,0:T(8,128)(2,1)S(1)}, u32[]{:S(2)}, u32[]{:S(2)}) collective-permute-start(bf16[368,128]{1,0:T(8,128)(2,1)} %get-tuple-element.74), channel_id=1, source_target_pairs={{0,64},{64,0},{1,65},{65,1},{2,66},{66,2},{3,67},{67,3},{4,68},{68... | collective-permute-start | bytes 282632 | tf_op jit(solution)/shard_map/ppermute | solution.py:34
  163.0 13.2 %collective-permute-start.32 = (bf16[736,128]{1,0:T(8,128)(2,1)S(1)}, bf16[736,128]{1,0:T(8,128)(2,1)S(1)}, u32[]{:S(2)}, u32[]{:S(2)}) collective-permute-start(bf16[736,128]{1,0:T(8,128)(2,1)S(1)} %pad_maximum_fusion.5), channel_id=1, source_target_pairs={{0,192},{64,128},{128,64},{192,0},{1,193},{65,129},{129,65},{193,1... | collective-permute-start | bytes 565256 | tf_op jit(solution)/shard_map/ppermute | solution.py:34
  163.7 11.8 %collective-permute-start.34 = (bf16[368,128]{1,0:T(8,128)(2,1)S(1)}, bf16[368,128]{1,0:T(8,128)(2,1)S(1)}, u32[]{:S(2)}, u32[]{:S(2)}) collective-permute-start(bf16[368,128]{1,0:T(8,128)(2,1)S(1)} %get-tuple-element.83), channel_id=1, source_target_pairs={{0,64},{64,0},{1,65},{65,1},{2,66},{66,2},{3,67},{67,3},{4,68},{68... | collective-permute-start | bytes 282632 | tf_op jit(solution)/shard_map/ppermute | solution.py:34
  165.6 9.8 %collective-permute-start.33 = (bf16[368,128]{1,0:T(8,128)(2,1)S(1)}, bf16[368,128]{1,0:T(8,128)(2,1)S(1)}, u32[]{:S(2)}, u32[]{:S(2)}) collective-permute-start(bf16[368,128]{1,0:T(8,128)(2,1)S(1)} %get-tuple-element.82), channel_id=1, source_target_pairs={{0,128},{128,0},{1,129},{129,1},{2,130},{130,2},{3,131},{131,3},{4... | collective-permute-start | bytes 282632 | tf_op jit(solution)/shard_map/ppermute | solution.py:34
  (25 other events, 277.6 us)

commit v2 on v1

--- a/solution.py
+++ b/solution.py
@@ -122,7 +122,7 @@
     count, width = rows.shape
     quarter = ours[0].shape[0]
     factor = 1.0 / float(width) ** 0.5
-    step, cut = 256, 3 * SLAB
+    step, cut = 512, 3 * SLAB
 
     def body(place, rows, far, far_across, near_k, *refs):
         blocks, (variance, rate, out, out_sq, ratio, slope, total, weights, held) = refs[:8], refs[8:]
@@ -179,7 +179,7 @@
 
 def statistic(ratio, slope, intensity, labels, ids, near, last):
     quarter, count = ratio.shape[0] // 2, ratio.shape[1]
-    steps = 4
+    steps = 2
 
     def body(*refs):
         ratio, slope = refs[0], refs[1] if slopes else None
@@ -194,13 +194,15 @@
                 value = (hot - expected) * 0.5 if slope is None else (hot + expected) * slope[here]
                 weight[here] = value.astype(BF)
 
-        joint[:, : 3 * SLAB] = near[...]
-        joint[:, 3 * SLAB :] = last[...]
+        for k in range(2):
+            joint[:, 4 * k * SLAB : (4 * k + 3) * SLAB] = near[:, 3 * k * SLAB : 3 * (k + 1) * SLAB]
+            joint[:, (4 * k + 3) * SLAB : 4 * (k + 1) * SLAB] = last[:, k * SLAB : (k + 1) * SLAB]
         sums = jnp.dot(weight[...], joint[...], preferred_element_type=F32)
         keep[...] = sums[:quarter]
         give[...] = sums[quarter:].astype(BF)
 
     slopes = [] if slope is None else [slope]
+    last = pltpu.with_memory_space_constraint(last, pltpu.HBM)
     given = [ratio, *slopes, intensity, labels, ids, near, last]
     block = lambda rows, cols: pl.BlockSpec((rows, cols), lambda i: (0, i))
     return stepped(
@@ -208,10 +210,10 @@
         "statistic",
         steps,
         given,
-        [whole(v) for v in given[:-2]] + [block(count, 3 * SLAB), block(count, SLAB)],
+        [whole(v) for v in given[:-2]] + [block(count, 6 * SLAB), block(count, 2 * SLAB)],
         [jax.ShapeDtypeStruct((quarter, 16 * SLAB), F32), jax.ShapeDtypeStruct((quarter, 16 * SLAB), BF)],
-        [block(quarter, 4 * SLAB), block(quarter, 4 * SLAB)],
-        [pltpu.VMEM(ratio.shape, BF), pltpu.VMEM((count, 4 * SLAB), BF)],
+        [block(quarter, 8 * SLAB), block(quarter, 8 * SLAB)],
+        [pltpu.VMEM(ratio.shape, BF), pltpu.VMEM((count, 8 * SLAB), BF)],
         2 * count * 16 * SLAB * 2 * quarter,
     )
 

time: 183 us -> 182 us (level)
    unnamed x30 -> x26, local copies, waits for them, and re-layouts: 8.36 us -> 7.15 us
where the time goes in v2:
time: 182 us; the launch traced here: 181 us
  waiting for transfers between devices  62.7 us (34%)
  starting transfers between devices  55.9 us (31%)
  Pallas kernels  38 us (21%)
  local copies, waits for them, and re-layouts  12.4 us (7%)
  other arithmetic  11 us (6%)
    ppermute x36, waiting for transfers between devices, swap(): return lax.ppermute(value, names, pairs)  55.9 us
    ppermute x36, starting transfers between devices, swap(): return lax.ppermute(value, names, pairs)  50.4 us
    pallas_call x4, Pallas kernels, stepped(): pl.pallas_call(body, grid=(steps,), out_shape=out_shape, in_specs=in_spec...  35.4 us
    unnamed x26, local copies, waits for them, and re-layouts  7.15 us
    all_to_all x1, waiting for transfers between devices, body(): lax.all_to_all(total, ('h', 'x', 'zl'), 0, 0, tiled=True)  6.84 us
    all_to_all x1, starting transfers between devices, body(): lax.all_to_all(total, ('h', 'x', 'zl'), 0, 0, tiled=True)  5.56 us
  transfers between devices with their start and end apart: 37, of which 20 were waited for; matrix products, arithmetic and copies ran while one was open for 7% of the time, Pallas kernels for 10%

profile of v2, /device:TPU:1, one launch (start us, length us, event | category | flops | bytes accessed | tf_op | source)
XLA Modules:
  0.0 181.2 jit_solution(13813940428019561286)
XLA Ops:
  1.2 2.6 %unit_slabs.1 = (bf16[128,1024]{1,0:T(8,128)(2,1)}, bf16[128,1024]{1,0:T(8,128)(2,1)}) custom-call(s32[2]{0:T(128)} %pad_add_fusion.1.at, bf16[256,1024]{1,0:T(8,128)(2,1)} %points.1, bf16[512,1024]{1,0:T(8,128)(2,1)} %feature.1), custom_call_target="tpu_custom_call" | custom-call | tf_op jit(solution)/shard_map/unit_slabs/pallas_call | solution.py:54
  5.7 3.3 %collective-permute-start.6 = (bf16[2,352,64]{2,1,0:T(8,128)(2,1)S(1)}, bf16[2,352,64]{2,1,0:T(8,128)(2,1)S(1)}, u32[]{:S(2)}, u32[]{:S(2)}) collective-permute-start(bf16[2,352,64]{2,1,0:T(8,128)(2,1)S(1)} %bitcast.108), channel_id=1, source_target_pairs={{0,8},{8,0},{1,9},{9,1},{2,10},{10,2},{3,11},{11,3},{4,12},{12,4},... | collective-permute-start | bytes 270344 | tf_op jit(solution)/shard_map/ppermute | solution.py:34
  9.1 2.9 %collective-permute-start = (bf16[128,1024]{1,0:T(8,128)(2,1)}, bf16[128,1024]{1,0:T(8,128)(2,1)S(1)}, u32[]{:S(2)}, u32[]{:S(2)}) collective-permute-start(bf16[128,1024]{1,0:T(8,128)(2,1)} %get-tuple-element.45), channel_id=1, source_target_pairs={{0,64},{64,0},{1,65},{65,1},{2,66},{66,2},{3,67},{67,3},{4,68},{68... | collective-permute-start | bytes 786440 | tf_op jit(solution)/shard_map/ppermute | solution.py:34
  14.2 4.5 %collective-permute-start.9 = (bf16[352,128]{1,0:T(8,128)(2,1)S(1)}, bf16[352,128]{1,0:T(8,128)(2,1)S(1)}, u32[]{:S(2)}, u32[]{:S(2)}) collective-permute-start(bf16[352,128]{1,0:T(8,128)(2,1)S(1)} %get-tuple-element.133), channel_id=1, source_target_pairs={{0,192},{64,128},{128,64},{192,0},{1,193},{65,129},{129,65},{193,1... | collective-permute-start | bytes 270344 | tf_op jit(solution)/shard_map/ppermute | solution.py:34
  19.9 4.6 %collective-permute-done.2 = bf16[128,1024]{1,0:T(8,128)(2,1)S(1)} collective-permute-done((bf16[128,1024]{1,0:T(8,128)(2,1)}, bf16[128,1024]{1,0:T(8,128)(2,1)S(1)}, u32[]{:S(2)}, u32[]{:S(2)}) %collective-permute-start.2) | collective-permute-done | bytes 262176 | tf_op jit(solution)/shard_map/ppermute | solution.py:34
  26.3 7.8 %collective-permute-done.8 = bf16[352,128]{1,0:T(8,128)(2,1)S(1)} collective-permute-done((bf16[352,128]{1,0:T(8,128)(2,1)S(1)}, bf16[352,128]{1,0:T(8,128)(2,1)S(1)}, u32[]{:S(2)}, u32[]{:S(2)}) %collective-permute-start.8) | collective-permute-done | bytes 90144 | tf_op jit(solution)/shard_map/ppermute | solution.py:34
  37.6 3.7 %collective-permute-done.5 = s32[512]{0:T(512)S(1)} collective-permute-done((s32[512]{0:T(512)S(1)}, s32[512]{0:T(512)S(1)}, u32[]{:S(2)}, u32[]{:S(2)}) %collective-permute-start.5) | collective-permute-done | bytes 2080 | tf_op jit(solution)/shard_map/ppermute | solution.py:34
  43.7 4.4 %collective-permute-done.1.relay_far = bf16[128,1024]{1,0:T(8,128)(2,1)S(1)} collective-permute-done((bf16[128,1024]{1,0:T(8,128)(2,1)S(1)}, bf16[128,1024]{1,0:T(8,128)(2,1)S(1)}, u32[]{:S(2)}, u32[]{:S(2)}) %collective-permute-start.1) | collective-permute-done | bytes 262176 | tf_op jit(solution)/shard_map/ppermute | solution.py:34
  48.8 4.2 %collective-permute-start.14 = (bf16[384,1024]{1,0:T(8,128)(2,1)S(1)}, bf16[384,1024]{1,0:T(8,128)(2,1)}, u32[]{:S(2)}, u32[]{:S(2)}) collective-permute-start(bf16[384,1024]{1,0:T(8,128)(2,1)S(1)} %collective-permute-done.3.near), channel_id=1, source_target_pairs={{0,8},{8,0},{1,9},{9,1},{2,10},{10,2},{3,11},{11,3},{4,12},{12,4},... | collective-permute-start | bytes 2359304 | tf_op jit(solution)/shard_map/ppermute | solution.py:34
  58.0 8.7 %near_rows.1 = (bf16[1024,1536]{1,0:T(8,128)(2,1)}, bf16[1024,1536]{1,0:T(8,128)(2,1)}, bf16[1024,1024]{1,0:T(8,128)(2,1)}) custom-call(s32[17]{0:T(128)S(1)} %stack.147.place, bf16[512,1024]{1,0:T(8,128)(2,1)S(1)} %copy-done.1, bf16[128,1024]{1,0:T(8,128)(2,1)S(1)} %collective-permute-done.relay, bf16[128,1024]{1,0:T(8,128)(2,1)S(1)} %copy-done.3, ...), custom_call_target="tpu_custom_call" | custom-call | flops 3221225472 | bytes 11534404 | tf_op jit(solution)/shard_map/near_rows/pallas_call | solution.py:63
  73.7 11.2 %means.1 = (bf16[1024,512]{1,0:T(8,128)(2,1)}, bf16[1024,512]{1,0:T(8,128)(2,1)}, f32[704,1024]{1,0:T(8,128)}, f32[704,1024]{1,0:T(8,128)}, f32[1,1024]{1,0:T(1,128)S(1)}) custom-call(s32[4]{0:T(128)S(1)} %pad_add_fusion.place, bf16[1024,1024]{1,0:T(8,128)(2,1)} %get-tuple-element.54.rows, bf16[256,1024]{1,0:T(8,128)(2,1)} %collective-permute-done.12.far, ...), custom_call_target="tpu_custom_call" | custom-call | flops 2952790016 | bytes 18355728 | tf_op jit(solution)/shard_map/means/pallas_call | solution.py:63
  85.5 5.6 %all-to-all-start = ((f32[16,8,128]{2,1,0:T(8,128)}), f32[16,8,128]{2,1,0:T(8,128)S(1)}, u32[]{:S(2)}, u32[]{:S(2)}) async-start(f32[16,8,128]{2,1,0:T(8,128)} %tile.9), calls=%async_computation | async-start | bytes 131072 | tf_op jit(solution)/shard_map/all_to_all | solution.py:280
  91.3 6.8 %all-to-all-done = f32[16,8,128]{2,1,0:T(8,128)S(1)} async-done(((f32[16,8,128]{2,1,0:T(8,128)}), f32[16,8,128]{2,1,0:T(8,128)S(1)}, u32[]{:S(2)}, u32[]{:S(2)}) %all-to-all-start) | async-done | bytes 65568 | tf_op jit(solution)/shard_map/all_to_all | solution.py:280
  98.2 6.9 %statistic.2 = (f32[352,2048]{1,0:T(8,128)S(1)}, bf16[352,2048]{1,0:T(8,128)(2,1)S(1)}) custom-call(f32[704,1024]{1,0:T(8,128)} %get-tuple-element.60.refs_0_, f32[1,1024]{1,0:T(1,128)S(1)} %bitcast.101, s32[1,1024]{1,0:T(1,128)S(1)} %broadcast_select_fusion.refs_2_.refs_3_, s32[704,1]{1,0:T(8,128)S(1)} %add.323.refs_3_.refs_4_, ...), custom_call_target="tpu_custom_call" | custom-call | flops 2952790016 | bytes 11283200 | tf_op jit(solution)/shard_map/statistic/pallas_call | solution.py:63
  107.1 8.6 %statistic.3 = (f32[352,2048]{1,0:T(8,128)S(1)}, bf16[352,2048]{1,0:T(8,128)(2,1)}) custom-call(f32[704,1024]{1,0:T(8,128)} %get-tuple-element.60.refs_0_, f32[704,1024]{1,0:T(8,128)} %get-tuple-element.66.refs_1_, f32[1,1024]{1,0:T(1,128)S(1)} %bitcast.102, s32[1,1024]{1,0:T(1,128)S(1)} %broadcast_select_fusion.refs_2_.refs_3_, ...), custom_call_target="tpu_custom_call" | custom-call | flops 2952790016 | bytes 14166784 | tf_op jit(solution)/shard_map/statistic/pallas_call | solution.py:63
  118.9 2.6 %collective-permute-start.23 = (bf16[352,512]{1,0:T(8,128)(2,1)}, bf16[352,512]{1,0:T(8,128)(2,1)}, u32[]{:S(2)}, u32[]{:S(2)}) collective-permute-start(bf16[352,512]{1,0:T(8,128)(2,1)} %get-tuple-element.99), channel_id=1, source_target_pairs={{0,32},{16,48},{32,0},{48,16},{1,33},{17,49},{33,1},{49,17},{2,34}... | collective-permute-start | bytes 1081352 | tf_op jit(solution)/shard_map/ppermute | solution.py:34
  121.7 2.4 %add_convert_fusion = (bf16[352,512]{1,0:T(8,128)(2,1)}, bf16[352,512]{1,0:T(8,128)(2,1)}, bf16[352,512]{1,0:T(8,128)(2,1)}) fusion(f32[352,2048]{1,0:T(8,128)S(1)} %get-tuple-element.69, bf16[352,2048]{1,0:T(8,128)(2,1)} %collective-permute-done.24), kind=kLoop, calls=%fused_computation.8 | loop fusion | flops 1622016 | bytes 4325376 | tf_op jit(solution)/shard_map/convert_element_type | solution.py:316
  124.2 2.4 %collective-permute-start.28 = (bf16[352,512]{1,0:T(8,128)(2,1)}, bf16[352,512]{1,0:T(8,128)(2,1)}, u32[]{:S(2)}, u32[]{:S(2)}) collective-permute-start(bf16[352,512]{1,0:T(8,128)(2,1)} %get-tuple-element.96), channel_id=1, source_target_pairs={{0,48},{16,32},{32,16},{48,0},{1,49},{17,33},{33,17},{49,1},{2,50}... | collective-permute-start | bytes 1081352 | tf_op jit(solution)/shard_map/ppermute | solution.py:34
  128.2 9.9 %collective-permute-done.23 = bf16[352,512]{1,0:T(8,128)(2,1)} collective-permute-done((bf16[352,512]{1,0:T(8,128)(2,1)}, bf16[352,512]{1,0:T(8,128)(2,1)}, u32[]{:S(2)}, u32[]{:S(2)}) %collective-permute-start.23) | collective-permute-done | bytes 360480 | tf_op jit(solution)/shard_map/ppermute | solution.py:34
  143.6 6.7 %collective-permute-start.30 = (bf16[368,128]{1,0:T(8,128)(2,1)}, bf16[368,128]{1,0:T(8,128)(2,1)S(1)}, u32[]{:S(2)}, u32[]{:S(2)}) collective-permute-start(bf16[368,128]{1,0:T(8,128)(2,1)} %get-tuple-element.73), channel_id=1, source_target_pairs={{0,128},{128,0},{1,129},{129,1},{2,130},{130,2},{3,131},{131,3},{4... | collective-permute-start | bytes 282632 | tf_op jit(solution)/shard_map/ppermute | solution.py:34
  150.8 4.8 %collective-permute-done.28 = bf16[352,512]{1,0:T(8,128)(2,1)} collective-permute-done((bf16[352,512]{1,0:T(8,128)(2,1)}, bf16[352,512]{1,0:T(8,128)(2,1)}, u32[]{:S(2)}, u32[]{:S(2)}) %collective-permute-start.28) | collective-permute-done | bytes 360480 | tf_op jit(solution)/shard_map/ppermute | solution.py:34
  155.6 4.4 %collective-permute-done.31 = bf16[368,128]{1,0:T(8,128)(2,1)S(1)} collective-permute-done((bf16[368,128]{1,0:T(8,128)(2,1)}, bf16[368,128]{1,0:T(8,128)(2,1)S(1)}, u32[]{:S(2)}, u32[]{:S(2)}) %collective-permute-start.31) | collective-permute-done | bytes 94240 | tf_op jit(solution)/shard_map/ppermute | solution.py:34
  164.5 3.0 %collective-permute-start.33 = (bf16[368,128]{1,0:T(8,128)(2,1)S(1)}, bf16[368,128]{1,0:T(8,128)(2,1)S(1)}, u32[]{:S(2)}, u32[]{:S(2)}) collective-permute-start(bf16[368,128]{1,0:T(8,128)(2,1)S(1)} %get-tuple-element.82), channel_id=1, source_target_pairs={{0,128},{128,0},{1,129},{129,1},{2,130},{130,2},{3,131},{131,3},{4... | collective-permute-start | bytes 282632 | tf_op jit(solution)/shard_map/ppermute | solution.py:34
  168.6 5.7 %collective-permute-done.33 = bf16[368,128]{1,0:T(8,128)(2,1)S(1)} collective-permute-done((bf16[368,128]{1,0:T(8,128)(2,1)S(1)}, bf16[368,128]{1,0:T(8,128)(2,1)S(1)}, u32[]{:S(2)}, u32[]{:S(2)}) %collective-permute-start.33) | collective-permute-done | bytes 94240 | tf_op jit(solution)/shard_map/ppermute | solution.py:34
  (150 shorter events, 52.2 us)
Async XLA Ops:
  9.0 15.4 %collective-permute-start.2 = (bf16[128,1024]{1,0:T(8,128)(2,1)}, bf16[128,1024]{1,0:T(8,128)(2,1)S(1)}, u32[]{:S(2)}, u32[]{:S(2)}) collective-permute-start(bf16[128,1024]{1,0:T(8,128)(2,1)} %get-tuple-element.46), channel_id=1, source_target_pairs={{0,1},{1,0},{2,3},{3,2},{4,5},{5,4},{6,7},{7,6},{8,9},{9,8},{10,11... | collective-permute-start | bytes 786440 | tf_op jit(solution)/shard_map/ppermute | solution.py:34
  9.1 16.2 %collective-permute-start = (bf16[128,1024]{1,0:T(8,128)(2,1)}, bf16[128,1024]{1,0:T(8,128)(2,1)S(1)}, u32[]{:S(2)}, u32[]{:S(2)}) collective-permute-start(bf16[128,1024]{1,0:T(8,128)(2,1)} %get-tuple-element.45), channel_id=1, source_target_pairs={{0,64},{64,0},{1,65},{65,1},{2,66},{66,2},{3,67},{67,3},{4,68},{68... | collective-permute-start | bytes 786440 | tf_op jit(solution)/shard_map/ppermute | solution.py:34
  14.1 12.2 %collective-permute-start.7 = (bf16[352,128]{1,0:T(8,128)(2,1)S(1)}, bf16[352,128]{1,0:T(8,128)(2,1)S(1)}, u32[]{:S(2)}, u32[]{:S(2)}) collective-permute-start(bf16[352,128]{1,0:T(8,128)(2,1)S(1)} %get-tuple-element.133), channel_id=1, source_target_pairs={{0,64},{64,0},{1,65},{65,1},{2,66},{66,2},{3,67},{67,3},{4,68},{68... | collective-permute-start | bytes 270344 | tf_op jit(solution)/shard_map/ppermute | solution.py:34
  14.2 19.9 %collective-permute-start.9 = (bf16[352,128]{1,0:T(8,128)(2,1)S(1)}, bf16[352,128]{1,0:T(8,128)(2,1)S(1)}, u32[]{:S(2)}, u32[]{:S(2)}) collective-permute-start(bf16[352,128]{1,0:T(8,128)(2,1)S(1)} %get-tuple-element.133), channel_id=1, source_target_pairs={{0,192},{64,128},{128,64},{192,0},{1,193},{65,129},{129,65},{193,1... | collective-permute-start | bytes 270344 | tf_op jit(solution)/shard_map/ppermute | solution.py:34
  18.7 15.4 %collective-permute-start.8 = (bf16[352,128]{1,0:T(8,128)(2,1)S(1)}, bf16[352,128]{1,0:T(8,128)(2,1)S(1)}, u32[]{:S(2)}, u32[]{:S(2)}) collective-permute-start(bf16[352,128]{1,0:T(8,128)(2,1)S(1)} %bitcast.106), channel_id=1, source_target_pairs={{0,128},{128,0},{1,129},{129,1},{2,130},{130,2},{3,131},{131,3},{4... | collective-permute-start | bytes 270344 | tf_op jit(solution)/shard_map/ppermute | solution.py:34
  25.9 22.9 %collective-permute-start.3 = (bf16[384,1024]{1,0:T(8,128)(2,1)}, bf16[384,1024]{1,0:T(8,128)(2,1)S(1)}, u32[]{:S(2)}, u32[]{:S(2)}) collective-permute-start(bf16[384,1024]{1,0:T(8,128)(2,1)} %constant_dynamic-update-slice_fusion), channel_id=1, source_target_pairs={{0,2},{2,0},{4,6},{6,4},{1,3},{3,1},{5,7},{7,5},{8,10},{10,8},{12,... | collective-permute-start | bytes 2359304 | tf_op jit(solution)/shard_map/ppermute | solution.py:34
  25.9 22.9 %collective-permute-start.4 = (bf16[384,1024]{1,0:T(8,128)(2,1)}, bf16[384,1024]{1,0:T(8,128)(2,1)}, u32[]{:S(2)}, u32[]{:S(2)}) collective-permute-start(bf16[384,1024]{1,0:T(8,128)(2,1)} %constant_dynamic-update-slice_fusion), channel_id=1, source_target_pairs={{0,6},{2,4},{4,2},{6,0},{1,7},{3,5},{5,3},{7,1},{8,14},{10,12},{12... | collective-permute-start | bytes 2359304 | tf_op jit(solution)/shard_map/ppermute | solution.py:34
  34.3 14.6 %collective-permute-start.10 = (bf16[352,512]{1,0:T(8,128)(2,1)S(1)}, bf16[352,512]{1,0:T(8,128)(2,1)}, u32[]{:S(2)}, u32[]{:S(2)}) collective-permute-start(bf16[352,512]{1,0:T(8,128)(2,1)S(1)} %pad_maximum_fusion.4.refs_0_), channel_id=1, source_target_pairs={{0,16},{16,0},{32,48},{48,32},{1,17},{17,1},{33,49},{49,33},{2,18}... | collective-permute-start | bytes 1081352 | tf_op jit(solution)/shard_map/ppermute | solution.py:34
  35.6 13.2 %collective-permute-start.11 = (bf16[352,512]{1,0:T(8,128)(2,1)S(1)}, bf16[352,512]{1,0:T(8,128)(2,1)}, u32[]{:S(2)}, u32[]{:S(2)}) collective-permute-start(bf16[352,512]{1,0:T(8,128)(2,1)S(1)} %pad_maximum_fusion.4.refs_0_), channel_id=1, source_target_pairs={{0,48},{16,32},{32,16},{48,0},{1,49},{17,33},{33,17},{49,1},{2,50}... | collective-permute-start | bytes 1081352 | tf_op jit(solution)/shard_map/ppermute | solution.py:34
  53.9 15.2 %collective-permute-start.12 = (bf16[256,1024]{1,0:T(8,128)(2,1)S(1)}, bf16[256,1024]{1,0:T(8,128)(2,1)}, u32[]{:S(2)}, u32[]{:S(2)}) collective-permute-start(bf16[256,1024]{1,0:T(8,128)(2,1)S(1)} %pad_maximum_fusion.2.pair), channel_id=1, source_target_pairs={{0,4},{2,6},{4,0},{6,2},{1,5},{3,7},{5,1},{7,3},{8,12},{10,14},{12... | collective-permute-start | bytes 1572872 | tf_op jit(solution)/shard_map/ppermute | solution.py:34
  56.0 14.6 %collective-permute-start.17 = (bf16[352,512]{1,0:T(8,128)(2,1)S(1)}, bf16[352,512]{1,0:T(8,128)(2,1)}, u32[]{:S(2)}, u32[]{:S(2)}) collective-permute-start(bf16[352,512]{1,0:T(8,128)(2,1)S(1)} %pad_maximum_fusion.4.refs_0_), channel_id=1, source_target_pairs={{0,32},{16,48},{32,0},{48,16},{1,33},{17,49},{33,1},{49,17},{2,34}... | collective-permute-start | bytes 1081352 | tf_op jit(solution)/shard_map/ppermute | solution.py:34
  85.5 12.7 %all-to-all-start = ((f32[16,8,128]{2,1,0:T(8,128)}), f32[16,8,128]{2,1,0:T(8,128)S(1)}, u32[]{:S(2)}, u32[]{:S(2)}) async-start(f32[16,8,128]{2,1,0:T(8,128)} %tile.9), calls=%async_computation | async-start | bytes 131072 | tf_op jit(solution)/shard_map/all_to_all | solution.py:280
  105.1 11.3 %collective-permute-start.22 = (bf16[352,2048]{1,0:T(8,128)(2,1)S(1)}, bf16[352,2048]{1,0:T(8,128)(2,1)S(1)}, u32[]{:S(2)}, u32[]{:S(2)}) collective-permute-start(bf16[352,2048]{1,0:T(8,128)(2,1)S(1)} %get-tuple-element.65), channel_id=1, source_target_pairs={{0,8},{8,0},{1,9},{9,1},{2,10},{10,2},{3,11},{11,3},{4,12},{12,4},... | collective-permute-start | bytes 4325384 | tf_op jit(solution)/shard_map/ppermute | solution.py:34
  117.9 10.4 %collective-permute-start.25 = (bf16[352,512]{1,0:T(8,128)(2,1)}, bf16[352,512]{1,0:T(8,128)(2,1)S(1)}, u32[]{:S(2)}, u32[]{:S(2)}) collective-permute-start(bf16[352,512]{1,0:T(8,128)(2,1)} %get-tuple-element.101), channel_id=1, source_target_pairs={{0,16},{16,0},{32,48},{48,32},{1,17},{17,1},{33,49},{49,33},{2,18}... | collective-permute-start | bytes 1081352 | tf_op jit(solution)/shard_map/ppermute | solution.py:34
  118.9 19.3 %collective-permute-start.23 = (bf16[352,512]{1,0:T(8,128)(2,1)}, bf16[352,512]{1,0:T(8,128)(2,1)}, u32[]{:S(2)}, u32[]{:S(2)}) collective-permute-start(bf16[352,512]{1,0:T(8,128)(2,1)} %get-tuple-element.99), channel_id=1, source_target_pairs={{0,32},{16,48},{32,0},{48,16},{1,33},{17,49},{33,1},{49,17},{2,34}... | collective-permute-start | bytes 1081352 | tf_op jit(solution)/shard_map/ppermute | solution.py:34
  121.5 18.7 %collective-permute-start.26 = (bf16[352,512]{1,0:T(8,128)(2,1)}, bf16[352,512]{1,0:T(8,128)(2,1)}, u32[]{:S(2)}, u32[]{:S(2)}) collective-permute-start(bf16[352,512]{1,0:T(8,128)(2,1)} %get-tuple-element.100), channel_id=1, source_target_pairs={{0,48},{16,32},{32,16},{48,0},{1,49},{17,33},{33,17},{49,1},{2,50}... | collective-permute-start | bytes 1081352 | tf_op jit(solution)/shard_map/ppermute | solution.py:34
  124.2 26.6 %collective-permute-start.27 = (bf16[352,512]{1,0:T(8,128)(2,1)}, bf16[352,512]{1,0:T(8,128)(2,1)}, u32[]{:S(2)}, u32[]{:S(2)}) collective-permute-start(bf16[352,512]{1,0:T(8,128)(2,1)} %get-tuple-element.97), channel_id=1, source_target_pairs={{0,16},{16,0},{32,48},{48,32},{1,17},{17,1},{33,49},{49,33},{2,18}... | collective-permute-start | bytes 1081352 | tf_op jit(solution)/shard_map/ppermute | solution.py:34
  124.2 31.4 %collective-permute-start.28 = (bf16[352,512]{1,0:T(8,128)(2,1)}, bf16[352,512]{1,0:T(8,128)(2,1)}, u32[]{:S(2)}, u32[]{:S(2)}) collective-permute-start(bf16[352,512]{1,0:T(8,128)(2,1)} %get-tuple-element.96), channel_id=1, source_target_pairs={{0,48},{16,32},{32,16},{48,0},{1,49},{17,33},{33,17},{49,1},{2,50}... | collective-permute-start | bytes 1081352 | tf_op jit(solution)/shard_map/ppermute | solution.py:34
  141.9 18.1 %collective-permute-start.29 = (bf16[352,512]{1,0:T(8,128)(2,1)}, bf16[352,512]{1,0:T(8,128)(2,1)S(1)}, u32[]{:S(2)}, u32[]{:S(2)}) collective-permute-start(bf16[352,512]{1,0:T(8,128)(2,1)} %get-tuple-element.72), channel_id=1, source_target_pairs={{0,32},{16,48},{32,0},{48,16},{1,33},{17,49},{33,1},{49,17},{2,34}... | collective-permute-start | bytes 1081352 | tf_op jit(solution)/shard_map/ppermute | solution.py:34
  143.6 12.0 %collective-permute-start.30 = (bf16[368,128]{1,0:T(8,128)(2,1)}, bf16[368,128]{1,0:T(8,128)(2,1)S(1)}, u32[]{:S(2)}, u32[]{:S(2)}) collective-permute-start(bf16[368,128]{1,0:T(8,128)(2,1)} %get-tuple-element.73), channel_id=1, source_target_pairs={{0,128},{128,0},{1,129},{129,1},{2,130},{130,2},{3,131},{131,3},{4... | collective-permute-start | bytes 282632 | tf_op jit(solution)/shard_map/ppermute | solution.py:34
  150.3 9.6 %collective-permute-start.31 = (bf16[368,128]{1,0:T(8,128)(2,1)}, bf16[368,128]{1,0:T(8,128)(2,1)S(1)}, u32[]{:S(2)}, u32[]{:S(2)}) collective-permute-start(bf16[368,128]{1,0:T(8,128)(2,1)} %get-tuple-element.74), channel_id=1, source_target_pairs={{0,64},{64,0},{1,65},{65,1},{2,66},{66,2},{3,67},{67,3},{4,68},{68... | collective-permute-start | bytes 282632 | tf_op jit(solution)/shard_map/ppermute | solution.py:34
  161.8 13.3 %collective-permute-start.32 = (bf16[736,128]{1,0:T(8,128)(2,1)S(1)}, bf16[736,128]{1,0:T(8,128)(2,1)S(1)}, u32[]{:S(2)}, u32[]{:S(2)}) collective-permute-start(bf16[736,128]{1,0:T(8,128)(2,1)S(1)} %pad_maximum_fusion.5), channel_id=1, source_target_pairs={{0,192},{64,128},{128,64},{192,0},{1,193},{65,129},{129,65},{193,1... | collective-permute-start | bytes 565256 | tf_op jit(solution)/shard_map/ppermute | solution.py:34
  162.6 11.7 %collective-permute-start.34 = (bf16[368,128]{1,0:T(8,128)(2,1)S(1)}, bf16[368,128]{1,0:T(8,128)(2,1)S(1)}, u32[]{:S(2)}, u32[]{:S(2)}) collective-permute-start(bf16[368,128]{1,0:T(8,128)(2,1)S(1)} %get-tuple-element.83), channel_id=1, source_target_pairs={{0,64},{64,0},{1,65},{65,1},{2,66},{66,2},{3,67},{67,3},{4,68},{68... | collective-permute-start | bytes 282632 | tf_op jit(solution)/shard_map/ppermute | solution.py:34
  164.5 9.8 %collective-permute-start.33 = (bf16[368,128]{1,0:T(8,128)(2,1)S(1)}, bf16[368,128]{1,0:T(8,128)(2,1)S(1)}, u32[]{:S(2)}, u32[]{:S(2)}) collective-permute-start(bf16[368,128]{1,0:T(8,128)(2,1)S(1)} %get-tuple-element.82), channel_id=1, source_target_pairs={{0,128},{128,0},{1,129},{129,1},{2,130},{130,2},{3,131},{131,3},{4... | collective-permute-start | bytes 282632 | tf_op jit(solution)/shard_map/ppermute | solution.py:34
  (23 other events, 267.3 us)

commit v3 on v2

--- a/solution.py
+++ b/solution.py
@@ -122,7 +122,7 @@
     count, width = rows.shape
     quarter = ours[0].shape[0]
     factor = 1.0 / float(width) ** 0.5
-    step, cut = 512, 3 * SLAB
+    step, cut = 256, 3 * SLAB
 
     def body(place, rows, far, far_across, near_k, *refs):
         blocks, (variance, rate, out, out_sq, ratio, slope, total, weights, held) = refs[:8], refs[8:]

time: 182 us -> 181 us (level)
  no operation moved by 1% of the time
where the time goes in v3:
time: 181 us
  waiting for transfers between devices  62.7 us (35%)
  starting transfers between devices  56 us (31%)
  Pallas kernels  37.8 us (21%)
  local copies, waits for them, and re-layouts  12.4 us (7%)
  other arithmetic  11 us (6%)
    ppermute x36, waiting for transfers between devices, swap(): return lax.ppermute(value, names, pairs)  55.9 us
    ppermute x36, starting transfers between devices, swap(): return lax.ppermute(value, names, pairs)  50.4 us
    pallas_call x4, Pallas kernels, stepped(): pl.pallas_call(body, grid=(steps,), out_shape=out_shape, in_specs=in_spec...  35.2 us
    unnamed x26, local copies, waits for them, and re-layouts  7.15 us
    all_to_all x1, waiting for transfers between devices, body(): lax.all_to_all(total, ('h', 'x', 'zl'), 0, 0, tiled=True)  6.83 us
    all_to_all x1, starting transfers between devices, body(): lax.all_to_all(total, ('h', 'x', 'zl'), 0, 0, tiled=True)  5.56 us
  transfers between devices with their start and end apart: 37, of which 20 were waited for; matrix products, arithmetic and copies ran while one was open for 7% of the time, Pallas kernels for 10%

profile of v3, /device:TPU:1, one launch (start us, length us, event | category | flops | bytes accessed | tf_op | source)
XLA Modules:
  0.0 181.0 jit_solution(17096900170706701832)
XLA Ops:
  1.2 2.6 %unit_slabs.1 = (bf16[128,1024]{1,0:T(8,128)(2,1)}, bf16[128,1024]{1,0:T(8,128)(2,1)}) custom-call(s32[2]{0:T(128)} %pad_add_fusion.1.at, bf16[256,1024]{1,0:T(8,128)(2,1)} %points.1, bf16[512,1024]{1,0:T(8,128)(2,1)} %feature.1), custom_call_target="tpu_custom_call" | custom-call | tf_op jit(solution)/shard_map/unit_slabs/pallas_call | solution.py:54
  5.7 3.3 %collective-permute-start.6 = (bf16[2,352,64]{2,1,0:T(8,128)(2,1)S(1)}, bf16[2,352,64]{2,1,0:T(8,128)(2,1)S(1)}, u32[]{:S(2)}, u32[]{:S(2)}) collective-permute-start(bf16[2,352,64]{2,1,0:T(8,128)(2,1)S(1)} %bitcast.108), channel_id=1, source_target_pairs={{0,8},{8,0},{1,9},{9,1},{2,10},{10,2},{3,11},{11,3},{4,12},{12,4},... | collective-permute-start | bytes 270344 | tf_op jit(solution)/shard_map/ppermute | solution.py:34
  9.1 2.9 %collective-permute-start = (bf16[128,1024]{1,0:T(8,128)(2,1)}, bf16[128,1024]{1,0:T(8,128)(2,1)S(1)}, u32[]{:S(2)}, u32[]{:S(2)}) collective-permute-start(bf16[128,1024]{1,0:T(8,128)(2,1)} %get-tuple-element.45), channel_id=1, source_target_pairs={{0,64},{64,0},{1,65},{65,1},{2,66},{66,2},{3,67},{67,3},{4,68},{68... | collective-permute-start | bytes 786440 | tf_op jit(solution)/shard_map/ppermute | solution.py:34
  14.2 4.5 %collective-permute-start.9 = (bf16[352,128]{1,0:T(8,128)(2,1)S(1)}, bf16[352,128]{1,0:T(8,128)(2,1)S(1)}, u32[]{:S(2)}, u32[]{:S(2)}) collective-permute-start(bf16[352,128]{1,0:T(8,128)(2,1)S(1)} %get-tuple-element.133), channel_id=1, source_target_pairs={{0,192},{64,128},{128,64},{192,0},{1,193},{65,129},{129,65},{193,1... | collective-permute-start | bytes 270344 | tf_op jit(solution)/shard_map/ppermute | solution.py:34
  19.9 4.6 %collective-permute-done.2 = bf16[128,1024]{1,0:T(8,128)(2,1)S(1)} collective-permute-done((bf16[128,1024]{1,0:T(8,128)(2,1)}, bf16[128,1024]{1,0:T(8,128)(2,1)S(1)}, u32[]{:S(2)}, u32[]{:S(2)}) %collective-permute-start.2) | collective-permute-done | bytes 262176 | tf_op jit(solution)/shard_map/ppermute | solution.py:34
  26.3 7.8 %collective-permute-done.8 = bf16[352,128]{1,0:T(8,128)(2,1)S(1)} collective-permute-done((bf16[352,128]{1,0:T(8,128)(2,1)S(1)}, bf16[352,128]{1,0:T(8,128)(2,1)S(1)}, u32[]{:S(2)}, u32[]{:S(2)}) %collective-permute-start.8) | collective-permute-done | bytes 90144 | tf_op jit(solution)/shard_map/ppermute | solution.py:34
  37.6 3.7 %collective-permute-done.5 = s32[512]{0:T(512)S(1)} collective-permute-done((s32[512]{0:T(512)S(1)}, s32[512]{0:T(512)S(1)}, u32[]{:S(2)}, u32[]{:S(2)}) %collective-permute-start.5) | collective-permute-done | bytes 2080 | tf_op jit(solution)/shard_map/ppermute | solution.py:34
  43.7 4.4 %collective-permute-done.1.relay_far = bf16[128,1024]{1,0:T(8,128)(2,1)S(1)} collective-permute-done((bf16[128,1024]{1,0:T(8,128)(2,1)S(1)}, bf16[128,1024]{1,0:T(8,128)(2,1)S(1)}, u32[]{:S(2)}, u32[]{:S(2)}) %collective-permute-start.1) | collective-permute-done | bytes 262176 | tf_op jit(solution)/shard_map/ppermute | solution.py:34
  48.8 4.2 %collective-permute-start.14 = (bf16[384,1024]{1,0:T(8,128)(2,1)S(1)}, bf16[384,1024]{1,0:T(8,128)(2,1)}, u32[]{:S(2)}, u32[]{:S(2)}) collective-permute-start(bf16[384,1024]{1,0:T(8,128)(2,1)S(1)} %collective-permute-done.3.near), channel_id=1, source_target_pairs={{0,8},{8,0},{1,9},{9,1},{2,10},{10,2},{3,11},{11,3},{4,12},{12,4},... | collective-permute-start | bytes 2359304 | tf_op jit(solution)/shard_map/ppermute | solution.py:34
  58.0 8.7 %near_rows.1 = (bf16[1024,1536]{1,0:T(8,128)(2,1)}, bf16[1024,1536]{1,0:T(8,128)(2,1)}, bf16[1024,1024]{1,0:T(8,128)(2,1)}) custom-call(s32[17]{0:T(128)S(1)} %stack.147.place, bf16[512,1024]{1,0:T(8,128)(2,1)S(1)} %copy-done.1, bf16[128,1024]{1,0:T(8,128)(2,1)S(1)} %collective-permute-done.relay, bf16[128,1024]{1,0:T(8,128)(2,1)S(1)} %copy-done.3, ...), custom_call_target="tpu_custom_call" | custom-call | flops 3221225472 | bytes 11534404 | tf_op jit(solution)/shard_map/near_rows/pallas_call | solution.py:63
  73.7 10.9 %means.1 = (bf16[1024,512]{1,0:T(8,128)(2,1)}, bf16[1024,512]{1,0:T(8,128)(2,1)}, f32[704,1024]{1,0:T(8,128)}, f32[704,1024]{1,0:T(8,128)}, f32[1,1024]{1,0:T(1,128)S(1)}) custom-call(s32[4]{0:T(128)S(1)} %pad_add_fusion.place, bf16[1024,1024]{1,0:T(8,128)(2,1)} %get-tuple-element.54.rows, bf16[256,1024]{1,0:T(8,128)(2,1)} %collective-permute-done.12.far, ...), custom_call_target="tpu_custom_call" | custom-call | flops 2952790016 | bytes 18355728 | tf_op jit(solution)/shard_map/means/pallas_call | solution.py:63
  85.2 5.6 %all-to-all-start = ((f32[16,8,128]{2,1,0:T(8,128)}), f32[16,8,128]{2,1,0:T(8,128)S(1)}, u32[]{:S(2)}, u32[]{:S(2)}) async-start(f32[16,8,128]{2,1,0:T(8,128)} %tile.9), calls=%async_computation | async-start | bytes 131072 | tf_op jit(solution)/shard_map/all_to_all | solution.py:280
  91.0 6.8 %all-to-all-done = f32[16,8,128]{2,1,0:T(8,128)S(1)} async-done(((f32[16,8,128]{2,1,0:T(8,128)}), f32[16,8,128]{2,1,0:T(8,128)S(1)}, u32[]{:S(2)}, u32[]{:S(2)}) %all-to-all-start) | async-done | bytes 65568 | tf_op jit(solution)/shard_map/all_to_all | solution.py:280
  97.9 6.9 %statistic.2 = (f32[352,2048]{1,0:T(8,128)S(1)}, bf16[352,2048]{1,0:T(8,128)(2,1)S(1)}) custom-call(f32[704,1024]{1,0:T(8,128)} %get-tuple-element.60.refs_0_, f32[1,1024]{1,0:T(1,128)S(1)} %bitcast.101, s32[1,1024]{1,0:T(1,128)S(1)} %broadcast_select_fusion.refs_2_.refs_3_, s32[704,1]{1,0:T(8,128)S(1)} %add.323.refs_3_.refs_4_, ...), custom_call_target="tpu_custom_call" | custom-call | flops 2952790016 | bytes 11283200 | tf_op jit(solution)/shard_map/statistic/pallas_call | solution.py:63
  106.7 8.6 %statistic.3 = (f32[352,2048]{1,0:T(8,128)S(1)}, bf16[352,2048]{1,0:T(8,128)(2,1)}) custom-call(f32[704,1024]{1,0:T(8,128)} %get-tuple-element.60.refs_0_, f32[704,1024]{1,0:T(8,128)} %get-tuple-element.66.refs_1_, f32[1,1024]{1,0:T(1,128)S(1)} %bitcast.102, s32[1,1024]{1,0:T(1,128)S(1)} %broadcast_select_fusion.refs_2_.refs_3_, ...), custom_call_target="tpu_custom_call" | custom-call | flops 2952790016 | bytes 14166784 | tf_op jit(solution)/shard_map/statistic/pallas_call | solution.py:63
  118.6 2.6 %collective-permute-start.23 = (bf16[352,512]{1,0:T(8,128)(2,1)}, bf16[352,512]{1,0:T(8,128)(2,1)}, u32[]{:S(2)}, u32[]{:S(2)}) collective-permute-start(bf16[352,512]{1,0:T(8,128)(2,1)} %get-tuple-element.99), channel_id=1, source_target_pairs={{0,32},{16,48},{32,0},{48,16},{1,33},{17,49},{33,1},{49,17},{2,34}... | collective-permute-start | bytes 1081352 | tf_op jit(solution)/shard_map/ppermute | solution.py:34
  121.5 2.4 %add_convert_fusion = (bf16[352,512]{1,0:T(8,128)(2,1)}, bf16[352,512]{1,0:T(8,128)(2,1)}, bf16[352,512]{1,0:T(8,128)(2,1)}) fusion(f32[352,2048]{1,0:T(8,128)S(1)} %get-tuple-element.69, bf16[352,2048]{1,0:T(8,128)(2,1)} %collective-permute-done.24), kind=kLoop, calls=%fused_computation.8 | loop fusion | flops 1622016 | bytes 4325376 | tf_op jit(solution)/shard_map/convert_element_type | solution.py:316
  123.9 2.4 %collective-permute-start.28 = (bf16[352,512]{1,0:T(8,128)(2,1)}, bf16[352,512]{1,0:T(8,128)(2,1)}, u32[]{:S(2)}, u32[]{:S(2)}) collective-permute-start(bf16[352,512]{1,0:T(8,128)(2,1)} %get-tuple-element.96), channel_id=1, source_target_pairs={{0,48},{16,32},{32,16},{48,0},{1,49},{17,33},{33,17},{49,1},{2,50}... | collective-permute-start | bytes 1081352 | tf_op jit(solution)/shard_map/ppermute | solution.py:34
  128.0 9.9 %collective-permute-done.23 = bf16[352,512]{1,0:T(8,128)(2,1)} collective-permute-done((bf16[352,512]{1,0:T(8,128)(2,1)}, bf16[352,512]{1,0:T(8,128)(2,1)}, u32[]{:S(2)}, u32[]{:S(2)}) %collective-permute-start.23) | collective-permute-done | bytes 360480 | tf_op jit(solution)/shard_map/ppermute | solution.py:34
  143.4 6.7 %collective-permute-start.30 = (bf16[368,128]{1,0:T(8,128)(2,1)}, bf16[368,128]{1,0:T(8,128)(2,1)S(1)}, u32[]{:S(2)}, u32[]{:S(2)}) collective-permute-start(bf16[368,128]{1,0:T(8,128)(2,1)} %get-tuple-element.73), channel_id=1, source_target_pairs={{0,128},{128,0},{1,129},{129,1},{2,130},{130,2},{3,131},{131,3},{4... | collective-permute-start | bytes 282632 | tf_op jit(solution)/shard_map/ppermute | solution.py:34
  150.6 4.8 %collective-permute-done.28 = bf16[352,512]{1,0:T(8,128)(2,1)} collective-permute-done((bf16[352,512]{1,0:T(8,128)(2,1)}, bf16[352,512]{1,0:T(8,128)(2,1)}, u32[]{:S(2)}, u32[]{:S(2)}) %collective-permute-start.28) | collective-permute-done | bytes 360480 | tf_op jit(solution)/shard_map/ppermute | solution.py:34
  155.4 4.4 %collective-permute-done.31 = bf16[368,128]{1,0:T(8,128)(2,1)S(1)} collective-permute-done((bf16[368,128]{1,0:T(8,128)(2,1)}, bf16[368,128]{1,0:T(8,128)(2,1)S(1)}, u32[]{:S(2)}, u32[]{:S(2)}) %collective-permute-start.31) | collective-permute-done | bytes 94240 | tf_op jit(solution)/shard_map/ppermute | solution.py:34
  164.3 3.0 %collective-permute-start.33 = (bf16[368,128]{1,0:T(8,128)(2,1)S(1)}, bf16[368,128]{1,0:T(8,128)(2,1)S(1)}, u32[]{:S(2)}, u32[]{:S(2)}) collective-permute-start(bf16[368,128]{1,0:T(8,128)(2,1)S(1)} %get-tuple-element.82), channel_id=1, source_target_pairs={{0,128},{128,0},{1,129},{129,1},{2,130},{130,2},{3,131},{131,3},{4... | collective-permute-start | bytes 282632 | tf_op jit(solution)/shard_map/ppermute | solution.py:34
  168.3 5.7 %collective-permute-done.33 = bf16[368,128]{1,0:T(8,128)(2,1)S(1)} collective-permute-done((bf16[368,128]{1,0:T(8,128)(2,1)S(1)}, bf16[368,128]{1,0:T(8,128)(2,1)S(1)}, u32[]{:S(2)}, u32[]{:S(2)}) %collective-permute-start.33) | collective-permute-done | bytes 94240 | tf_op jit(solution)/shard_map/ppermute | solution.py:34
  (150 shorter events, 52.2 us)
Async XLA Ops:
  9.0 15.4 %collective-permute-start.2 = (bf16[128,1024]{1,0:T(8,128)(2,1)}, bf16[128,1024]{1,0:T(8,128)(2,1)S(1)}, u32[]{:S(2)}, u32[]{:S(2)}) collective-permute-start(bf16[128,1024]{1,0:T(8,128)(2,1)} %get-tuple-element.46), channel_id=1, source_target_pairs={{0,1},{1,0},{2,3},{3,2},{4,5},{5,4},{6,7},{7,6},{8,9},{9,8},{10,11... | collective-permute-start | bytes 786440 | tf_op jit(solution)/shard_map/ppermute | solution.py:34
  9.1 16.2 %collective-permute-start = (bf16[128,1024]{1,0:T(8,128)(2,1)}, bf16[128,1024]{1,0:T(8,128)(2,1)S(1)}, u32[]{:S(2)}, u32[]{:S(2)}) collective-permute-start(bf16[128,1024]{1,0:T(8,128)(2,1)} %get-tuple-element.45), channel_id=1, source_target_pairs={{0,64},{64,0},{1,65},{65,1},{2,66},{66,2},{3,67},{67,3},{4,68},{68... | collective-permute-start | bytes 786440 | tf_op jit(solution)/shard_map/ppermute | solution.py:34
  14.1 12.2 %collective-permute-start.7 = (bf16[352,128]{1,0:T(8,128)(2,1)S(1)}, bf16[352,128]{1,0:T(8,128)(2,1)S(1)}, u32[]{:S(2)}, u32[]{:S(2)}) collective-permute-start(bf16[352,128]{1,0:T(8,128)(2,1)S(1)} %get-tuple-element.133), channel_id=1, source_target_pairs={{0,64},{64,0},{1,65},{65,1},{2,66},{66,2},{3,67},{67,3},{4,68},{68... | collective-permute-start | bytes 270344 | tf_op jit(solution)/shard_map/ppermute | solution.py:34
  14.2 19.9 %collective-permute-start.9 = (bf16[352,128]{1,0:T(8,128)(2,1)S(1)}, bf16[352,128]{1,0:T(8,128)(2,1)S(1)}, u32[]{:S(2)}, u32[]{:S(2)}) collective-permute-start(bf16[352,128]{1,0:T(8,128)(2,1)S(1)} %get-tuple-element.133), channel_id=1, source_target_pairs={{0,192},{64,128},{128,64},{192,0},{1,193},{65,129},{129,65},{193,1... | collective-permute-start | bytes 270344 | tf_op jit(solution)/shard_map/ppermute | solution.py:34
  18.7 15.4 %collective-permute-start.8 = (bf16[352,128]{1,0:T(8,128)(2,1)S(1)}, bf16[352,128]{1,0:T(8,128)(2,1)S(1)}, u32[]{:S(2)}, u32[]{:S(2)}) collective-permute-start(bf16[352,128]{1,0:T(8,128)(2,1)S(1)} %bitcast.106), channel_id=1, source_target_pairs={{0,128},{128,0},{1,129},{129,1},{2,130},{130,2},{3,131},{131,3},{4... | collective-permute-start | bytes 270344 | tf_op jit(solution)/shard_map/ppermute | solution.py:34
  25.9 22.9 %collective-permute-start.3 = (bf16[384,1024]{1,0:T(8,128)(2,1)}, bf16[384,1024]{1,0:T(8,128)(2,1)S(1)}, u32[]{:S(2)}, u32[]{:S(2)}) collective-permute-start(bf16[384,1024]{1,0:T(8,128)(2,1)} %constant_dynamic-update-slice_fusion), channel_id=1, source_target_pairs={{0,2},{2,0},{4,6},{6,4},{1,3},{3,1},{5,7},{7,5},{8,10},{10,8},{12,... | collective-permute-start | bytes 2359304 | tf_op jit(solution)/shard_map/ppermute | solution.py:34
  25.9 22.9 %collective-permute-start.4 = (bf16[384,1024]{1,0:T(8,128)(2,1)}, bf16[384,1024]{1,0:T(8,128)(2,1)}, u32[]{:S(2)}, u32[]{:S(2)}) collective-permute-start(bf16[384,1024]{1,0:T(8,128)(2,1)} %constant_dynamic-update-slice_fusion), channel_id=1, source_target_pairs={{0,6},{2,4},{4,2},{6,0},{1,7},{3,5},{5,3},{7,1},{8,14},{10,12},{12... | collective-permute-start | bytes 2359304 | tf_op jit(solution)/shard_map/ppermute | solution.py:34
  34.3 14.6 %collective-permute-start.10 = (bf16[352,512]{1,0:T(8,128)(2,1)S(1)}, bf16[352,512]{1,0:T(8,128)(2,1)}, u32[]{:S(2)}, u32[]{:S(2)}) collective-permute-start(bf16[352,512]{1,0:T(8,128)(2,1)S(1)} %pad_maximum_fusion.4.refs_0_), channel_id=1, source_target_pairs={{0,16},{16,0},{32,48},{48,32},{1,17},{17,1},{33,49},{49,33},{2,18}... | collective-permute-start | bytes 1081352 | tf_op jit(solution)/shard_map/ppermute | solution.py:34
  35.6 13.2 %collective-permute-start.11 = (bf16[352,512]{1,0:T(8,128)(2,1)S(1)}, bf16[352,512]{1,0:T(8,128)(2,1)}, u32[]{:S(2)}, u32[]{:S(2)}) collective-permute-start(bf16[352,512]{1,0:T(8,128)(2,1)S(1)} %pad_maximum_fusion.4.refs_0_), channel_id=1, source_target_pairs={{0,48},{16,32},{32,16},{48,0},{1,49},{17,33},{33,17},{49,1},{2,50}... | collective-permute-start | bytes 1081352 | tf_op jit(solution)/shard_map/ppermute | solution.py:34
  53.9 15.2 %collective-permute-start.12 = (bf16[256,1024]{1,0:T(8,128)(2,1)S(1)}, bf16[256,1024]{1,0:T(8,128)(2,1)}, u32[]{:S(2)}, u32[]{:S(2)}) collective-permute-start(bf16[256,1024]{1,0:T(8,128)(2,1)S(1)} %pad_maximum_fusion.2.pair), channel_id=1, source_target_pairs={{0,4},{2,6},{4,0},{6,2},{1,5},{3,7},{5,1},{7,3},{8,12},{10,14},{12... | collective-permute-start | bytes 1572872 | tf_op jit(solution)/shard_map/ppermute | solution.py:34
  56.0 14.6 %collective-permute-start.17 = (bf16[352,512]{1,0:T(8,128)(2,1)S(1)}, bf16[352,512]{1,0:T(8,128)(2,1)}, u32[]{:S(2)}, u32[]{:S(2)}) collective-permute-start(bf16[352,512]{1,0:T(8,128)(2,1)S(1)} %pad_maximum_fusion.4.refs_0_), channel_id=1, source_target_pairs={{0,32},{16,48},{32,0},{48,16},{1,33},{17,49},{33,1},{49,17},{2,34}... | collective-permute-start | bytes 1081352 | tf_op jit(solution)/shard_map/ppermute | solution.py:34
  85.2 12.7 %all-to-all-start = ((f32[16,8,128]{2,1,0:T(8,128)}), f32[16,8,128]{2,1,0:T(8,128)S(1)}, u32[]{:S(2)}, u32[]{:S(2)}) async-start(f32[16,8,128]{2,1,0:T(8,128)} %tile.9), calls=%async_computation | async-start | bytes 131072 | tf_op jit(solution)/shard_map/all_to_all | solution.py:280
  104.9 11.3 %collective-permute-start.22 = (bf16[352,2048]{1,0:T(8,128)(2,1)S(1)}, bf16[352,2048]{1,0:T(8,128)(2,1)S(1)}, u32[]{:S(2)}, u32[]{:S(2)}) collective-permute-start(bf16[352,2048]{1,0:T(8,128)(2,1)S(1)} %get-tuple-element.65), channel_id=1, source_target_pairs={{0,8},{8,0},{1,9},{9,1},{2,10},{10,2},{3,11},{11,3},{4,12},{12,4},... | collective-permute-start | bytes 4325384 | tf_op jit(solution)/shard_map/ppermute | solution.py:34
  117.6 10.4 %collective-permute-start.25 = (bf16[352,512]{1,0:T(8,128)(2,1)}, bf16[352,512]{1,0:T(8,128)(2,1)S(1)}, u32[]{:S(2)}, u32[]{:S(2)}) collective-permute-start(bf16[352,512]{1,0:T(8,128)(2,1)} %get-tuple-element.101), channel_id=1, source_target_pairs={{0,16},{16,0},{32,48},{48,32},{1,17},{17,1},{33,49},{49,33},{2,18}... | collective-permute-start | bytes 1081352 | tf_op jit(solution)/shard_map/ppermute | solution.py:34
  118.6 19.3 %collective-permute-start.23 = (bf16[352,512]{1,0:T(8,128)(2,1)}, bf16[352,512]{1,0:T(8,128)(2,1)}, u32[]{:S(2)}, u32[]{:S(2)}) collective-permute-start(bf16[352,512]{1,0:T(8,128)(2,1)} %get-tuple-element.99), channel_id=1, source_target_pairs={{0,32},{16,48},{32,0},{48,16},{1,33},{17,49},{33,1},{49,17},{2,34}... | collective-permute-start | bytes 1081352 | tf_op jit(solution)/shard_map/ppermute | solution.py:34
  121.3 18.7 %collective-permute-start.26 = (bf16[352,512]{1,0:T(8,128)(2,1)}, bf16[352,512]{1,0:T(8,128)(2,1)}, u32[]{:S(2)}, u32[]{:S(2)}) collective-permute-start(bf16[352,512]{1,0:T(8,128)(2,1)} %get-tuple-element.100), channel_id=1, source_target_pairs={{0,48},{16,32},{32,16},{48,0},{1,49},{17,33},{33,17},{49,1},{2,50}... | collective-permute-start | bytes 1081352 | tf_op jit(solution)/shard_map/ppermute | solution.py:34
  123.9 26.6 %collective-permute-start.27 = (bf16[352,512]{1,0:T(8,128)(2,1)}, bf16[352,512]{1,0:T(8,128)(2,1)}, u32[]{:S(2)}, u32[]{:S(2)}) collective-permute-start(bf16[352,512]{1,0:T(8,128)(2,1)} %get-tuple-element.97), channel_id=1, source_target_pairs={{0,16},{16,0},{32,48},{48,32},{1,17},{17,1},{33,49},{49,33},{2,18}... | collective-permute-start | bytes 1081352 | tf_op jit(solution)/shard_map/ppermute | solution.py:34
  123.9 31.4 %collective-permute-start.28 = (bf16[352,512]{1,0:T(8,128)(2,1)}, bf16[352,512]{1,0:T(8,128)(2,1)}, u32[]{:S(2)}, u32[]{:S(2)}) collective-permute-start(bf16[352,512]{1,0:T(8,128)(2,1)} %get-tuple-element.96), channel_id=1, source_target_pairs={{0,48},{16,32},{32,16},{48,0},{1,49},{17,33},{33,17},{49,1},{2,50}... | collective-permute-start | bytes 1081352 | tf_op jit(solution)/shard_map/ppermute | solution.py:34
  141.7 18.1 %collective-permute-start.29 = (bf16[352,512]{1,0:T(8,128)(2,1)}, bf16[352,512]{1,0:T(8,128)(2,1)S(1)}, u32[]{:S(2)}, u32[]{:S(2)}) collective-permute-start(bf16[352,512]{1,0:T(8,128)(2,1)} %get-tuple-element.72), channel_id=1, source_target_pairs={{0,32},{16,48},{32,0},{48,16},{1,33},{17,49},{33,1},{49,17},{2,34}... | collective-permute-start | bytes 1081352 | tf_op jit(solution)/shard_map/ppermute | solution.py:34
  143.4 12.0 %collective-permute-start.30 = (bf16[368,128]{1,0:T(8,128)(2,1)}, bf16[368,128]{1,0:T(8,128)(2,1)S(1)}, u32[]{:S(2)}, u32[]{:S(2)}) collective-permute-start(bf16[368,128]{1,0:T(8,128)(2,1)} %get-tuple-element.73), channel_id=1, source_target_pairs={{0,128},{128,0},{1,129},{129,1},{2,130},{130,2},{3,131},{131,3},{4... | collective-permute-start | bytes 282632 | tf_op jit(solution)/shard_map/ppermute | solution.py:34
  150.1 9.6 %collective-permute-start.31 = (bf16[368,128]{1,0:T(8,128)(2,1)}, bf16[368,128]{1,0:T(8,128)(2,1)S(1)}, u32[]{:S(2)}, u32[]{:S(2)}) collective-permute-start(bf16[368,128]{1,0:T(8,128)(2,1)} %get-tuple-element.74), channel_id=1, source_target_pairs={{0,64},{64,0},{1,65},{65,1},{2,66},{66,2},{3,67},{67,3},{4,68},{68... | collective-permute-start | bytes 282632 | tf_op jit(solution)/shard_map/ppermute | solution.py:34
  161.6 13.3 %collective-permute-start.32 = (bf16[736,128]{1,0:T(8,128)(2,1)S(1)}, bf16[736,128]{1,0:T(8,128)(2,1)S(1)}, u32[]{:S(2)}, u32[]{:S(2)}) collective-permute-start(bf16[736,128]{1,0:T(8,128)(2,1)S(1)} %pad_maximum_fusion.5), channel_id=1, source_target_pairs={{0,192},{64,128},{128,64},{192,0},{1,193},{65,129},{129,65},{193,1... | collective-permute-start | bytes 565256 | tf_op jit(solution)/shard_map/ppermute | solution.py:34
  162.4 11.7 %collective-permute-start.34 = (bf16[368,128]{1,0:T(8,128)(2,1)S(1)}, bf16[368,128]{1,0:T(8,128)(2,1)S(1)}, u32[]{:S(2)}, u32[]{:S(2)}) collective-permute-start(bf16[368,128]{1,0:T(8,128)(2,1)S(1)} %get-tuple-element.83), channel_id=1, source_target_pairs={{0,64},{64,0},{1,65},{65,1},{2,66},{66,2},{3,67},{67,3},{4,68},{68... | collective-permute-start | bytes 282632 | tf_op jit(solution)/shard_map/ppermute | solution.py:34
  164.3 9.8 %collective-permute-start.33 = (bf16[368,128]{1,0:T(8,128)(2,1)S(1)}, bf16[368,128]{1,0:T(8,128)(2,1)S(1)}, u32[]{:S(2)}, u32[]{:S(2)}) collective-permute-start(bf16[368,128]{1,0:T(8,128)(2,1)S(1)} %get-tuple-element.82), channel_id=1, source_target_pairs={{0,128},{128,0},{1,129},{129,1},{2,130},{130,2},{3,131},{131,3},{4... | collective-permute-start | bytes 282632 | tf_op jit(solution)/shard_map/ppermute | solution.py:34
  (23 other events, 267.6 us)
